TPU v7x, 256 devices: a whole 4x4x8 slice. The times are simulated.
256 devices in a mesh: leaf: 16 (over y, x), far: 16 (over z, core).
Axes of the slice: x: 4, y: 4, z: 8, core: 2. Of those that a mesh axis runs over, the one named last changes fastest.
Arguments:
- right_sides: bfloat16 [16, 64, 131072], P('far', None, 'leaf'), may hold values from -6 to 6
- point_coords: bfloat16 [16, 3, 131072], P('far', None, 'leaf'), may hold values from 0 to 1
- near_offsets: int32 [16, 1024, 24], P('far', 'leaf'), may hold values from -16 to 16
- leaf_basis: bfloat16 [16, 64, 131072], P('far', None, 'leaf'), may hold values from -0.5 to 0.5
- local_transfer: bfloat16 [16, 2016, 64, 64], P('far', 'leaf'), may hold values from -0.75 to 0.75
- top_transfer: bfloat16 [16, 30, 64, 64], P('far'), may hold values from -0.75 to 0.75
- coupling_pattern: int32 [16, 1008, 4], P('far', 'leaf'), may hold values from 0 to 15, all different within a row; in each aligned block of 63 rows (0 to 62, 63 to 125, ..., all dimensions but the last counted through in order) at most 32 rows name the same one
- coupling_blocks: bfloat16 [16, 1008, 4, 64, 64], P('far', 'leaf'), may hold values from -0.375 to 0.375
- root_pattern: int32 [16, 16], P('far'), may hold values 0 or 1
- root_blocks: bfloat16 [16, 16, 64, 64], P('far'), may hold values from -0.25 to 0.25
Outputs:
- potential: bfloat16 [16, 64, 131072], P('far', None, 'leaf')
Inputs may be any that keep to these rules, and one draw needn't show every extreme that they name: `coupling_pattern`: each row names 4 different partitions; among the rows of one subtree no partition is named more than 32 times, a bound that some block reaches.
All inputs are finite; a program needn't handle non-finite values. No bound on the sum of `root_pattern` on one device may be relied on, other than what follows from the above.
Results may differ from a plain program's by a relative error of at most 0.028.
Values may be sent and summed in bfloat16 or wider, within the bound.
A program may use at most 128 MiB of HBM per device.

v0:
```python
import math

import jax
import jax.numpy as jnp
from jax import lax
from jax.sharding import PartitionSpec as P

HALO = 16


HALF_ROOT = 0.7071067811865476
SOFTEN = 0.0004


def with_halo(array, sides, width):
    for axis, dim in sides:
        devices, length = (lax.axis_size(axis), array.shape[dim])
        up = [(i, (i + 1) % devices) for i in range(devices - 1)]
        down = [(j, i) for i, j in up]
        last = lax.slice_in_dim(array, length - width, length, axis=dim)
        initial = lax.slice_in_dim(array, 0, width, axis=dim)
        before = lax.ppermute(last, axis, up)
        after = lax.ppermute(initial, axis, down)
        array = jnp.concatenate([before, array, after], axis=dim)
    return array


def swapped(block, axis, stride):
    count = lax.axis_size(axis)
    route = []
    for low in range(count):
        high = low | 1 << stride
        if high != low and high < count:
            route += [(low, high), (high, low)]
    return lax.ppermute(block, axis, route)


def kernel_block(targets, sources, factor):
    squared = jnp.zeros(targets.shape[1:] + (sources.shape[2],), jnp.float32)
    for component in range(3):
        spacing = targets[component][:, :, None] - sources[component][:, None, :]
        squared = squared + spacing * spacing
    return (factor / jnp.sqrt(squared + SOFTEN)).astype(jnp.bfloat16)


def level_starts(first, levels):
    starts = []
    offset = 0
    for level_at in range(levels):
        starts.append(offset)
        offset = offset + (first >> level_at)
    return starts


def near_field(window, own_points, offsets, rhs_count, leaf_size):
    per_device = own_points.shape[1] // leaf_size
    margin = (window.shape[1] // leaf_size - per_device) // 2
    leaf_window_slice = window.reshape(window.shape[0], -1, leaf_size)
    targets = own_points.astype(jnp.float32).reshape(3, per_device, leaf_size)
    factor = 1.0 / math.sqrt(offsets.shape[1] * leaf_size)
    indices = jnp.arange(per_device, dtype=jnp.int32) + margin

    def advance(running, column):
        picked = jnp.take(leaf_window_slice, indices + column, axis=1)
        kernel = kernel_block(targets, picked[rhs_count:].astype(jnp.float32), factor)
        addend = jnp.einsum(
            "sib,iab->sia", picked[:rhs_count], kernel, preferred_element_type=jnp.float32
        )
        return (running + addend, None)

    running, unused = lax.scan(
        advance, jnp.zeros((rhs_count, per_device, leaf_size), jnp.float32), offsets.T
    )
    return running


def local(
    right_sides,
    point_coords,
    near_offsets,
    leaf_basis,
    local_transfer,
    top_transfer,
    coupling_pattern,
    coupling_blocks,
    root_pattern,
    root_blocks,
):
    rhs_count = right_sides.shape[1]
    rank_size = leaf_basis.shape[1]
    per_device = local_transfer.shape[1] // 2 + 1
    leaf_size = right_sides.shape[2] // per_device
    node_count = per_device - 1
    pair_count = coupling_pattern.shape[2]
    local_levels = per_device.bit_length() - 1
    subtree_count = lax.axis_size("leaf")
    top_levels = subtree_count.bit_length() - 1
    position = lax.axis_index("leaf")
    coef_width = rhs_count * rank_size
    point_values = right_sides[0]
    own_points = point_coords[0]
    stacked = jnp.concatenate([point_values, own_points], axis=0)
    window = with_halo(stacked, (("leaf", 1),), HALO * leaf_size)
    near_sum = near_field(window, own_points, near_offsets[0], rhs_count, leaf_size)
    leaf_window_slice = point_values.reshape(rhs_count, per_device, leaf_size)
    basis_window_slice = leaf_basis[0].reshape(rank_size, per_device, leaf_size)
    present_level_value = jnp.einsum(
        "ypb,kpb->pyk", leaf_window_slice, basis_window_slice, preferred_element_type=jnp.float32
    )
    transfer = local_transfer[0]
    local_starts = level_starts(per_device, local_levels)
    levels = []
    for level_at in range(local_levels):
        width_now = per_device >> level_at
        first_child = local_starts[level_at]
        mapped = jnp.einsum(
            "jsr,jrt->jst",
            present_level_value.astype(jnp.bfloat16),
            transfer[first_child : first_child + width_now],
            preferred_element_type=jnp.float32,
        )
        present_level_value = (mapped[0::2] + mapped[1::2]) * HALF_ROOT
        levels.append(present_level_value)
    node_coef = jnp.concatenate(levels, axis=0)
    tops = top_transfer[0]
    top_starts = level_starts(subtree_count, top_levels)
    present_level_value = node_coef[node_count - 1]
    for level_at in range(top_levels):
        matrix = lax.dynamic_index_in_dim(
            tops, top_starts[level_at] + (position >> level_at), 0, keepdims=False
        )
        mapped = jnp.dot(
            present_level_value.astype(jnp.bfloat16), matrix, preferred_element_type=jnp.float32
        )
        partner = swapped(mapped, "leaf", level_at)
        present_level_value = (mapped + partner) * HALF_ROOT
    partition_root = present_level_value
    every_root = lax.all_gather(partition_root[None], "far", axis=0, tiled=True)
    masked_roots = (
        every_root.astype(jnp.bfloat16) * root_pattern[0].astype(jnp.bfloat16)[:, None, None]
    )
    present_level_value = jnp.einsum(
        "psr,prt->st", masked_roots, root_blocks[0], preferred_element_type=jnp.float32
    )
    for level_at in reversed(range(top_levels)):
        matrix = lax.dynamic_index_in_dim(
            tops, top_starts[level_at] + (position >> level_at), 0, keepdims=False
        )
        present_level_value = jnp.dot(
            present_level_value.astype(jnp.bfloat16), matrix.T, preferred_element_type=jnp.float32
        )
    descent = present_level_value
    rounded = node_coef.astype(jnp.bfloat16).reshape(node_count, coef_width)
    pattern = coupling_pattern[0]
    every_node = lax.all_gather(rounded[None], "far", axis=0, tiled=True)
    flat_nodes = every_node.reshape(-1, coef_width)
    lookup = pattern * node_count + jnp.arange(node_count, dtype=jnp.int32)[:, None]
    sources = jnp.take(flat_nodes, lookup.reshape(-1), axis=0)
    sources = sources.reshape(node_count, pair_count, rhs_count, rank_size)
    gains = jnp.einsum(
        "jksr,jkrt->jst", sources, coupling_blocks[0], preferred_element_type=jnp.float32
    )
    node_starts = level_starts(per_device // 2, local_levels)
    present_level_value = descent[None]
    for level_at in range(local_levels, 0, -1):
        width_now = per_device >> level_at
        first_node = node_starts[level_at - 1]
        present_level_value = present_level_value + gains[first_node : first_node + width_now]
        first_child = local_starts[level_at - 1]
        doubled = jnp.repeat(present_level_value.astype(jnp.bfloat16), 2, axis=0)
        present_level_value = jnp.einsum(
            "jsr,jtr->jst",
            doubled,
            transfer[first_child : first_child + 2 * width_now],
            preferred_element_type=jnp.float32,
        )
    leaf_local_coef = present_level_value.astype(jnp.bfloat16)
    farfield_sum = jnp.einsum(
        "bhv,vbu->hbu", leaf_local_coef, basis_window_slice, preferred_element_type=jnp.float32
    )
    potential = (near_sum + farfield_sum).astype(jnp.bfloat16)
    return potential.reshape(1, rhs_count, per_device * leaf_size)


def solution(mesh):
    return jax.shard_map(
        local,
        mesh=mesh,
        in_specs=(
            P("far", None, "leaf"),
            P("far", None, "leaf"),
            P("far", "leaf", None),
            P("far", None, "leaf"),
            P("far", "leaf", None, None),
            P("far", None, None, None),
            P("far", "leaf", None),
            P("far", "leaf", None, None, None),
            P("far", None),
            P("far", None, None, None),
        ),
        out_specs=P("far", None, "leaf"),
        check_vma=False,
    )
```

profile of v0, /device:TPU:1, one launch (start us, length us, event | category | flops | bytes accessed | tf_op | source)
XLA Modules:
  0.0 429.7 jit_solution(10275503828086607319)
XLA Ops:
  6.5 2.7 slice.134
  16.3 2.3 copy.56
  18.6 2.7 copy.64
  21.3 4.5 %fusion.26 = f32[64,64,64]{2,1,0:T(8,128)} fusion(bf16[1,64,64,64]{3,2,1,0:T(8,128)(2,1)S(1)} %copy-done.4, bf16[64,64,128]{2,1,0:T(8,128)(2,1)} %bitcast.186, bf16[64,64,128]{2,1,0:T(8,128)(2,1)S(1)} %bitcast.179), kind=kOutput, calls=%fused_computation.42 | convolution fusion | flops 100925440 | bytes 3670016 | tf_op jit(solution)/shard_map/jsr,jrt->jst/dot_general | solution.py:116
  41.2 4.4 %concatenate.37 = bf16[1,63,4096]{2,1,0:T(8,128)(2,1)} concatenate(bf16[1,32,4096]{2,1,0:T(8,128)(2,1)S(1)} %concatenate.31, bf16[1,16,4096]{2,1,0:T(8,128)(2,1)} %concatenate.32, bf16[1,8,4096]{2,1,0:T(8,128)(2,1)S(1)} %concatenate.33, bf16[1,4,4096]{2,1,0:T(4,128)(2,1)} %concatenate.34, bf16[1,2,4096]{2,1,0:T(2,128)(2,1)S(1)} %concatenate.35, bf16[1,1,4096]{2,1,0:T(2,128)(2,1)} %concatenate.36), dimensions={1} | concatenate | bytes 1032192 | tf_op jit(solution)/shard_map/concatenate | solution.py:124
  51.0 4.5 %collective-permute-start.3 = (f32[64,64]{1,0:T(8,128)S(1)}, f32[64,64]{1,0:T(8,128)S(1)}, u32[]{:S(2)}, u32[]{:S(2)}) collective-permute-start(f32[64,64]{1,0:T(8,128)S(1)} %fusion.64), channel_id=1, source_target_pairs={{0,32},{32,0},{16,48},{48,16},{64,96},{96,64},{80,112},{112,80},{1... | collective-permute-start | bytes 49160 | tf_op jit(solution)/shard_map/ppermute | solution.py:35
  55.5 2.3 collective-permute-done.3
  58.0 3.2 collective-permute-start.4
  63.0 3.2 collective-permute-start.5
  67.6 25.5 %all-gather = bf16[1024,64]{1,0:T(8,128)(2,1)S(1)} all-gather(bf16[64,64]{1,0:T(8,128)(2,1)S(1)} %add_multiply_fusion), channel_id=2, replica_groups=mesh['leaf'=16,'far'=16] {'far'}, dimensions={0}, use_global_device_ids=true | all-gather | bytes 139264 | tf_op jit(solution)/shard_map/all_gather | solution.py:138
  98.7 285.0 %while.12 = (s32[]{:T(128)}, f32[64,64,128]{2,0,1:T(8,128)}, f32[3,64,128]{2,1,0:T(8,128)S(1)}, s32[24,64]{1,0:T(8,128)}, bf16[67,96,128]{2,0,1:T(8,128)(2,1)}, /*index=5*/s32[]{:T(128)}, s32[]{:T(128)}) while((s32[]{:T(128)}, f32[64,64,128]{2,0,1:T(8,128)}, f32[3,64,128]{2,1,0:T(8,128)S(1)}, s32[24,64]{1,0:T(8,128)}, ...), condition=%wide.region_1.2_spmd.clone.clone, body=%wide.region_0.1_spmd.clone.clone.sunk | while | flops 147375936 | bytes 10376671 | solution.py:71
  99.4 2.3 gather_fusion
  102.7 5.9 %bitcast_add_fusion.6 = f32[64,64,128]{2,0,1:T(8,128)} fusion(f32[64,64,128]{2,0,1:T(8,128)} %get-tuple-element.156, f32[64,128]{1,0:T(8,128)S(1)} %bitcast.193, f32[64,128]{1,0:T(8,128)S(1)} %get-tuple-element.143, f32[64,128]{1,0:T(8,128)S(1)} %bitcast.194, f32[64,128]{1,0:T(8,128)S(1)} %get-tuple-element.145, f32[64,128]{1,0:T(8,128)S(1)} %bitcast.192, ...), kind=kOutput, calls=%fused_computation.5.clone.1 | convolution fusion | flops 146800640 | bytes 5439489 | tf_op jit(solution)/shard_map/while/body/eval_jaxpr/sib,iab->sia/dot_general | solution.py:66
  112.7 8.0 %bitcast_add_fusion.6 = f32[64,64,128]{2,0,1:T(8,128)} fusion(f32[64,64,128]{2,0,1:T(8,128)} %get-tuple-element.156, f32[64,128]{1,0:T(8,128)S(1)} %bitcast.193, f32[64,128]{1,0:T(8,128)S(1)} %get-tuple-element.143, f32[64,128]{1,0:T(8,128)S(1)} %bitcast.194, f32[64,128]{1,0:T(8,128)S(1)} %get-tuple-element.145, f32[64,128]{1,0:T(8,128)S(1)} %bitcast.192, ...), kind=kOutput, calls=%fused_computation.5.clone.1 | convolution fusion | flops 146800640 | bytes 5439489 | tf_op jit(solution)/shard_map/while/body/eval_jaxpr/sib,iab->sia/dot_general | solution.py:66
  121.3 2.3 gather_fusion
  124.6 8.0 %bitcast_add_fusion.6 = f32[64,64,128]{2,0,1:T(8,128)} fusion(f32[64,64,128]{2,0,1:T(8,128)} %get-tuple-element.156, f32[64,128]{1,0:T(8,128)S(1)} %bitcast.193, f32[64,128]{1,0:T(8,128)S(1)} %get-tuple-element.143, f32[64,128]{1,0:T(8,128)S(1)} %bitcast.194, f32[64,128]{1,0:T(8,128)S(1)} %get-tuple-element.145, f32[64,128]{1,0:T(8,128)S(1)} %bitcast.192, ...), kind=kOutput, calls=%fused_computation.5.clone.1 | convolution fusion | flops 146800640 | bytes 5439489 | tf_op jit(solution)/shard_map/while/body/eval_jaxpr/sib,iab->sia/dot_general | solution.py:66
  136.6 8.0 %bitcast_add_fusion.6 = f32[64,64,128]{2,0,1:T(8,128)} fusion(f32[64,64,128]{2,0,1:T(8,128)} %get-tuple-element.156, f32[64,128]{1,0:T(8,128)S(1)} %bitcast.193, f32[64,128]{1,0:T(8,128)S(1)} %get-tuple-element.143, f32[64,128]{1,0:T(8,128)S(1)} %bitcast.194, f32[64,128]{1,0:T(8,128)S(1)} %get-tuple-element.145, f32[64,128]{1,0:T(8,128)S(1)} %bitcast.192, ...), kind=kOutput, calls=%fused_computation.5.clone.1 | convolution fusion | flops 146800640 | bytes 5439489 | tf_op jit(solution)/shard_map/while/body/eval_jaxpr/sib,iab->sia/dot_general | solution.py:66
  148.5 8.0 %bitcast_add_fusion.6 = f32[64,64,128]{2,0,1:T(8,128)} fusion(f32[64,64,128]{2,0,1:T(8,128)} %get-tuple-element.156, f32[64,128]{1,0:T(8,128)S(1)} %bitcast.193, f32[64,128]{1,0:T(8,128)S(1)} %get-tuple-element.143, f32[64,128]{1,0:T(8,128)S(1)} %bitcast.194, f32[64,128]{1,0:T(8,128)S(1)} %get-tuple-element.145, f32[64,128]{1,0:T(8,128)S(1)} %bitcast.192, ...), kind=kOutput, calls=%fused_computation.5.clone.1 | convolution fusion | flops 146800640 | bytes 5439489 | tf_op jit(solution)/shard_map/while/body/eval_jaxpr/sib,iab->sia/dot_general | solution.py:66
  157.2 2.3 gather_fusion
  160.5 8.0 %bitcast_add_fusion.6 = f32[64,64,128]{2,0,1:T(8,128)} fusion(f32[64,64,128]{2,0,1:T(8,128)} %get-tuple-element.156, f32[64,128]{1,0:T(8,128)S(1)} %bitcast.193, f32[64,128]{1,0:T(8,128)S(1)} %get-tuple-element.143, f32[64,128]{1,0:T(8,128)S(1)} %bitcast.194, f32[64,128]{1,0:T(8,128)S(1)} %get-tuple-element.145, f32[64,128]{1,0:T(8,128)S(1)} %bitcast.192, ...), kind=kOutput, calls=%fused_computation.5.clone.1 | convolution fusion | flops 146800640 | bytes 5439489 | tf_op jit(solution)/shard_map/while/body/eval_jaxpr/sib,iab->sia/dot_general | solution.py:66
  169.2 2.3 gather_fusion
  172.5 8.0 %bitcast_add_fusion.6 = f32[64,64,128]{2,0,1:T(8,128)} fusion(f32[64,64,128]{2,0,1:T(8,128)} %get-tuple-element.156, f32[64,128]{1,0:T(8,128)S(1)} %bitcast.193, f32[64,128]{1,0:T(8,128)S(1)} %get-tuple-element.143, f32[64,128]{1,0:T(8,128)S(1)} %bitcast.194, f32[64,128]{1,0:T(8,128)S(1)} %get-tuple-element.145, f32[64,128]{1,0:T(8,128)S(1)} %bitcast.192, ...), kind=kOutput, calls=%fused_computation.5.clone.1 | convolution fusion | flops 146800640 | bytes 5439489 | tf_op jit(solution)/shard_map/while/body/eval_jaxpr/sib,iab->sia/dot_general | solution.py:66
  184.4 8.0 %bitcast_add_fusion.6 = f32[64,64,128]{2,0,1:T(8,128)} fusion(f32[64,64,128]{2,0,1:T(8,128)} %get-tuple-element.156, f32[64,128]{1,0:T(8,128)S(1)} %bitcast.193, f32[64,128]{1,0:T(8,128)S(1)} %get-tuple-element.143, f32[64,128]{1,0:T(8,128)S(1)} %bitcast.194, f32[64,128]{1,0:T(8,128)S(1)} %get-tuple-element.145, f32[64,128]{1,0:T(8,128)S(1)} %bitcast.192, ...), kind=kOutput, calls=%fused_computation.5.clone.1 | convolution fusion | flops 146800640 | bytes 5439489 | tf_op jit(solution)/shard_map/while/body/eval_jaxpr/sib,iab->sia/dot_general | solution.py:66
  196.4 8.0 %bitcast_add_fusion.6 = f32[64,64,128]{2,0,1:T(8,128)} fusion(f32[64,64,128]{2,0,1:T(8,128)} %get-tuple-element.156, f32[64,128]{1,0:T(8,128)S(1)} %bitcast.193, f32[64,128]{1,0:T(8,128)S(1)} %get-tuple-element.143, f32[64,128]{1,0:T(8,128)S(1)} %bitcast.194, f32[64,128]{1,0:T(8,128)S(1)} %get-tuple-element.145, f32[64,128]{1,0:T(8,128)S(1)} %bitcast.192, ...), kind=kOutput, calls=%fused_computation.5.clone.1 | convolution fusion | flops 146800640 | bytes 5439489 | tf_op jit(solution)/shard_map/while/body/eval_jaxpr/sib,iab->sia/dot_general | solution.py:66
  205.1 2.3 gather_fusion
  208.3 8.0 %bitcast_add_fusion.6 = f32[64,64,128]{2,0,1:T(8,128)} fusion(f32[64,64,128]{2,0,1:T(8,128)} %get-tuple-element.156, f32[64,128]{1,0:T(8,128)S(1)} %bitcast.193, f32[64,128]{1,0:T(8,128)S(1)} %get-tuple-element.143, f32[64,128]{1,0:T(8,128)S(1)} %bitcast.194, f32[64,128]{1,0:T(8,128)S(1)} %get-tuple-element.145, f32[64,128]{1,0:T(8,128)S(1)} %bitcast.192, ...), kind=kOutput, calls=%fused_computation.5.clone.1 | convolution fusion | flops 146800640 | bytes 5439489 | tf_op jit(solution)/shard_map/while/body/eval_jaxpr/sib,iab->sia/dot_general | solution.py:66
  217.0 2.3 gather_fusion
  220.3 8.0 %bitcast_add_fusion.6 = f32[64,64,128]{2,0,1:T(8,128)} fusion(f32[64,64,128]{2,0,1:T(8,128)} %get-tuple-element.156, f32[64,128]{1,0:T(8,128)S(1)} %bitcast.193, f32[64,128]{1,0:T(8,128)S(1)} %get-tuple-element.143, f32[64,128]{1,0:T(8,128)S(1)} %bitcast.194, f32[64,128]{1,0:T(8,128)S(1)} %get-tuple-element.145, f32[64,128]{1,0:T(8,128)S(1)} %bitcast.192, ...), kind=kOutput, calls=%fused_computation.5.clone.1 | convolution fusion | flops 146800640 | bytes 5439489 | tf_op jit(solution)/shard_map/while/body/eval_jaxpr/sib,iab->sia/dot_general | solution.py:66
  232.3 8.0 %bitcast_add_fusion.6 = f32[64,64,128]{2,0,1:T(8,128)} fusion(f32[64,64,128]{2,0,1:T(8,128)} %get-tuple-element.156, f32[64,128]{1,0:T(8,128)S(1)} %bitcast.193, f32[64,128]{1,0:T(8,128)S(1)} %get-tuple-element.143, f32[64,128]{1,0:T(8,128)S(1)} %bitcast.194, f32[64,128]{1,0:T(8,128)S(1)} %get-tuple-element.145, f32[64,128]{1,0:T(8,128)S(1)} %bitcast.192, ...), kind=kOutput, calls=%fused_computation.5.clone.1 | convolution fusion | flops 146800640 | bytes 5439489 | tf_op jit(solution)/shard_map/while/body/eval_jaxpr/sib,iab->sia/dot_general | solution.py:66
  244.2 8.0 %bitcast_add_fusion.6 = f32[64,64,128]{2,0,1:T(8,128)} fusion(f32[64,64,128]{2,0,1:T(8,128)} %get-tuple-element.156, f32[64,128]{1,0:T(8,128)S(1)} %bitcast.193, f32[64,128]{1,0:T(8,128)S(1)} %get-tuple-element.143, f32[64,128]{1,0:T(8,128)S(1)} %bitcast.194, f32[64,128]{1,0:T(8,128)S(1)} %get-tuple-element.145, f32[64,128]{1,0:T(8,128)S(1)} %bitcast.192, ...), kind=kOutput, calls=%fused_computation.5.clone.1 | convolution fusion | flops 146800640 | bytes 5439489 | tf_op jit(solution)/shard_map/while/body/eval_jaxpr/sib,iab->sia/dot_general | solution.py:66
  256.2 8.0 %bitcast_add_fusion.6 = f32[64,64,128]{2,0,1:T(8,128)} fusion(f32[64,64,128]{2,0,1:T(8,128)} %get-tuple-element.156, f32[64,128]{1,0:T(8,128)S(1)} %bitcast.193, f32[64,128]{1,0:T(8,128)S(1)} %get-tuple-element.143, f32[64,128]{1,0:T(8,128)S(1)} %bitcast.194, f32[64,128]{1,0:T(8,128)S(1)} %get-tuple-element.145, f32[64,128]{1,0:T(8,128)S(1)} %bitcast.192, ...), kind=kOutput, calls=%fused_computation.5.clone.1 | convolution fusion | flops 146800640 | bytes 5439489 | tf_op jit(solution)/shard_map/while/body/eval_jaxpr/sib,iab->sia/dot_general | solution.py:66
  268.1 8.0 %bitcast_add_fusion.6 = f32[64,64,128]{2,0,1:T(8,128)} fusion(f32[64,64,128]{2,0,1:T(8,128)} %get-tuple-element.156, f32[64,128]{1,0:T(8,128)S(1)} %bitcast.193, f32[64,128]{1,0:T(8,128)S(1)} %get-tuple-element.143, f32[64,128]{1,0:T(8,128)S(1)} %bitcast.194, f32[64,128]{1,0:T(8,128)S(1)} %get-tuple-element.145, f32[64,128]{1,0:T(8,128)S(1)} %bitcast.192, ...), kind=kOutput, calls=%fused_computation.5.clone.1 | convolution fusion | flops 146800640 | bytes 5439489 | tf_op jit(solution)/shard_map/while/body/eval_jaxpr/sib,iab->sia/dot_general | solution.py:66
  280.1 8.0 %bitcast_add_fusion.6 = f32[64,64,128]{2,0,1:T(8,128)} fusion(f32[64,64,128]{2,0,1:T(8,128)} %get-tuple-element.156, f32[64,128]{1,0:T(8,128)S(1)} %bitcast.193, f32[64,128]{1,0:T(8,128)S(1)} %get-tuple-element.143, f32[64,128]{1,0:T(8,128)S(1)} %bitcast.194, f32[64,128]{1,0:T(8,128)S(1)} %get-tuple-element.145, f32[64,128]{1,0:T(8,128)S(1)} %bitcast.192, ...), kind=kOutput, calls=%fused_computation.5.clone.1 | convolution fusion | flops 146800640 | bytes 5439489 | tf_op jit(solution)/shard_map/while/body/eval_jaxpr/sib,iab->sia/dot_general | solution.py:66
  292.0 8.0 %bitcast_add_fusion.6 = f32[64,64,128]{2,0,1:T(8,128)} fusion(f32[64,64,128]{2,0,1:T(8,128)} %get-tuple-element.156, f32[64,128]{1,0:T(8,128)S(1)} %bitcast.193, f32[64,128]{1,0:T(8,128)S(1)} %get-tuple-element.143, f32[64,128]{1,0:T(8,128)S(1)} %bitcast.194, f32[64,128]{1,0:T(8,128)S(1)} %get-tuple-element.145, f32[64,128]{1,0:T(8,128)S(1)} %bitcast.192, ...), kind=kOutput, calls=%fused_computation.5.clone.1 | convolution fusion | flops 146800640 | bytes 5439489 | tf_op jit(solution)/shard_map/while/body/eval_jaxpr/sib,iab->sia/dot_general | solution.py:66
  300.7 2.3 gather_fusion
  304.0 8.0 %bitcast_add_fusion.6 = f32[64,64,128]{2,0,1:T(8,128)} fusion(f32[64,64,128]{2,0,1:T(8,128)} %get-tuple-element.156, f32[64,128]{1,0:T(8,128)S(1)} %bitcast.193, f32[64,128]{1,0:T(8,128)S(1)} %get-tuple-element.143, f32[64,128]{1,0:T(8,128)S(1)} %bitcast.194, f32[64,128]{1,0:T(8,128)S(1)} %get-tuple-element.145, f32[64,128]{1,0:T(8,128)S(1)} %bitcast.192, ...), kind=kOutput, calls=%fused_computation.5.clone.1 | convolution fusion | flops 146800640 | bytes 5439489 | tf_op jit(solution)/shard_map/while/body/eval_jaxpr/sib,iab->sia/dot_general | solution.py:66
  316.0 8.0 %bitcast_add_fusion.6 = f32[64,64,128]{2,0,1:T(8,128)} fusion(f32[64,64,128]{2,0,1:T(8,128)} %get-tuple-element.156, f32[64,128]{1,0:T(8,128)S(1)} %bitcast.193, f32[64,128]{1,0:T(8,128)S(1)} %get-tuple-element.143, f32[64,128]{1,0:T(8,128)S(1)} %bitcast.194, f32[64,128]{1,0:T(8,128)S(1)} %get-tuple-element.145, f32[64,128]{1,0:T(8,128)S(1)} %bitcast.192, ...), kind=kOutput, calls=%fused_computation.5.clone.1 | convolution fusion | flops 146800640 | bytes 5439489 | tf_op jit(solution)/shard_map/while/body/eval_jaxpr/sib,iab->sia/dot_general | solution.py:66
  327.9 8.0 %bitcast_add_fusion.6 = f32[64,64,128]{2,0,1:T(8,128)} fusion(f32[64,64,128]{2,0,1:T(8,128)} %get-tuple-element.156, f32[64,128]{1,0:T(8,128)S(1)} %bitcast.193, f32[64,128]{1,0:T(8,128)S(1)} %get-tuple-element.143, f32[64,128]{1,0:T(8,128)S(1)} %bitcast.194, f32[64,128]{1,0:T(8,128)S(1)} %get-tuple-element.145, f32[64,128]{1,0:T(8,128)S(1)} %bitcast.192, ...), kind=kOutput, calls=%fused_computation.5.clone.1 | convolution fusion | flops 146800640 | bytes 5439489 | tf_op jit(solution)/shard_map/while/body/eval_jaxpr/sib,iab->sia/dot_general | solution.py:66
  336.6 2.3 gather_fusion
  339.9 8.0 %bitcast_add_fusion.6 = f32[64,64,128]{2,0,1:T(8,128)} fusion(f32[64,64,128]{2,0,1:T(8,128)} %get-tuple-element.156, f32[64,128]{1,0:T(8,128)S(1)} %bitcast.193, f32[64,128]{1,0:T(8,128)S(1)} %get-tuple-element.143, f32[64,128]{1,0:T(8,128)S(1)} %bitcast.194, f32[64,128]{1,0:T(8,128)S(1)} %get-tuple-element.145, f32[64,128]{1,0:T(8,128)S(1)} %bitcast.192, ...), kind=kOutput, calls=%fused_computation.5.clone.1 | convolution fusion | flops 146800640 | bytes 5439489 | tf_op jit(solution)/shard_map/while/body/eval_jaxpr/sib,iab->sia/dot_general | solution.py:66
  351.8 8.0 %bitcast_add_fusion.6 = f32[64,64,128]{2,0,1:T(8,128)} fusion(f32[64,64,128]{2,0,1:T(8,128)} %get-tuple-element.156, f32[64,128]{1,0:T(8,128)S(1)} %bitcast.193, f32[64,128]{1,0:T(8,128)S(1)} %get-tuple-element.143, f32[64,128]{1,0:T(8,128)S(1)} %bitcast.194, f32[64,128]{1,0:T(8,128)S(1)} %get-tuple-element.145, f32[64,128]{1,0:T(8,128)S(1)} %bitcast.192, ...), kind=kOutput, calls=%fused_computation.5.clone.1 | convolution fusion | flops 146800640 | bytes 5439489 | tf_op jit(solution)/shard_map/while/body/eval_jaxpr/sib,iab->sia/dot_general | solution.py:66
  363.8 8.0 %bitcast_add_fusion.6 = f32[64,64,128]{2,0,1:T(8,128)} fusion(f32[64,64,128]{2,0,1:T(8,128)} %get-tuple-element.156, f32[64,128]{1,0:T(8,128)S(1)} %bitcast.193, f32[64,128]{1,0:T(8,128)S(1)} %get-tuple-element.143, f32[64,128]{1,0:T(8,128)S(1)} %bitcast.194, f32[64,128]{1,0:T(8,128)S(1)} %get-tuple-element.145, f32[64,128]{1,0:T(8,128)S(1)} %bitcast.192, ...), kind=kOutput, calls=%fused_computation.5.clone.1 | convolution fusion | flops 146800640 | bytes 5439489 | tf_op jit(solution)/shard_map/while/body/eval_jaxpr/sib,iab->sia/dot_general | solution.py:66
  375.8 8.0 %bitcast_add_fusion.6 = f32[64,64,128]{2,0,1:T(8,128)} fusion(f32[64,64,128]{2,0,1:T(8,128)} %get-tuple-element.156, f32[64,128]{1,0:T(8,128)S(1)} %bitcast.193, f32[64,128]{1,0:T(8,128)S(1)} %get-tuple-element.143, f32[64,128]{1,0:T(8,128)S(1)} %bitcast.194, f32[64,128]{1,0:T(8,128)S(1)} %get-tuple-element.145, f32[64,128]{1,0:T(8,128)S(1)} %bitcast.192, ...), kind=kOutput, calls=%fused_computation.5.clone.1 | convolution fusion | flops 146800640 | bytes 5439489 | tf_op jit(solution)/shard_map/while/body/eval_jaxpr/sib,iab->sia/dot_general | solution.py:66
  383.7 6.6 %reshape.230 = bf16[1008,4096]{1,0:T(8,128)(2,1)} reshape(bf16[16,63,4096]{2,1,0:T(8,128)(2,1)} %all-gather.3.cloned.1.call-done) | data formatting | bytes 16515072 | tf_op jit(solution)/shard_map/reshape | solution.py:156
  390.4 8.2 %gather_fusion.1 = bf16[252,4096]{1,0:T(8,128)(2,1)S(1)} fusion(bf16[1008,4096]{1,0:T(8,128)(2,1)} %reshape.230, s32[1024]{0:T(1024)S(1)} %pad_clamp_fusion.1), kind=kCustom, calls=%fused_computation.1 | custom fusion | bytes 4129776 | tf_op jit(solution)/shard_map/jit(_take)/gather | solution.py:158
  398.6 6.2 %gather.11 = bf16[63,4,64,64]{3,2,1,0:T(8,128)(2,1)} reshape(bf16[252,4096]{1,0:T(8,128)(2,1)S(1)} %gather_fusion.1) | data formatting | bytes 4128768 | tf_op jit(solution)/shard_map/jit(_take)/gather | solution.py:158
  404.8 4.9 %fusion.21 = f32[63,64,64]{2,1,0:T(8,128)S(1)} fusion(bf16[1,63,4,64,64]{4,3,2,1,0:T(8,128)(2,1)} %param.19, bf16[63,4,64,64]{3,2,1,0:T(8,128)(2,1)} %gather.11, pred[63,4]{1,0:T(8,128)(4,1)S(1)} %copy.51), kind=kOutput, calls=%fused_computation.39 | convolution fusion | flops 133152768 | bytes 5161212 | tf_op jit(solution)/shard_map/jksr,jkrt->jst/dot_general | solution.py:160
  415.1 4.6 %fusion.19 = bf16[64,64,128]{2,0,1:T(8,128)(2,1)} fusion(f32[64,64,128]{2,0,1:T(8,128)} %get-tuple-element.40, bf16[64,64,64]{2,1,0:T(8,128)(2,1)} %bitcast.187, bf16[1,64,64,64]{3,2,1,0:T(8,128)(2,1)S(1)} %copy-done.5, bf16[64,64,128]{2,1,0:T(8,128)(2,1)S(1)} %bitcast.180), kind=kOutput, calls=%fused_computation.36 | convolution fusion | flops 101974016 | bytes 5242880 | tf_op jit(solution)/shard_map/bhv,vbu->hbu/dot_general | solution.py:178
  (300 shorter events, 121.5 us)
Async XLA Ops:
  6.5 28.8 %copy-start = (bf16[1,30,64,64]{3,2,1,0:T(8,128)(2,1)S(1)}, bf16[1,30,64,64]{3,2,1,0:T(8,128)(2,1)}, u32[]{:S(2)}) copy-start(bf16[1,30,64,64]{3,2,1,0:T(8,128)(2,1)} %param.17) | copy-start | bytes 737284
  6.5 2.7 copy-start.1
  6.5 377.2 %all-gather.3.cloned.1.call-start = ((), (), s32[]{:S(2)}) async-start(), calls=%async_computation | async-start | bytes 8912896 | tf_op jit(solution)/shard_map/all_gather | solution.py:155
  16.3 5.0 %copy-start.2 = (bf16[8,8,64,128]{3,2,1,0:T(8,128)(2,1)}, bf16[8,8,64,128]{3,2,1,0:T(8,128)(2,1)S(1)}, u32[]{:S(2)}) copy-start(bf16[8,8,64,128]{3,2,1,0:T(8,128)(2,1)S(1)} %copy.65) | copy-start | bytes 3145732
  18.6 2.7 copy-start.4
  25.7 1.9 copy-start.9
  28.6 1.2 copy-start.7
  30.4 2.8 copy-start.10
  30.4 2.2 copy-start.8
  32.4 8.3 %copy-start.13 = (bf16[1,8,64,64]{3,2,1,0:T(8,128)(2,1)}, bf16[1,8,64,64]{3,2,1,0:T(8,128)(2,1)S(1)}, u32[]{:S(2)}) copy-start(bf16[1,8,64,64]{3,2,1,0:T(8,128)(2,1)S(1)} %copy.59) | copy-start | bytes 196612
  33.2 12.4 %copy-start.15 = (bf16[1,4,64,64]{3,2,1,0:T(8,128)(2,1)}, bf16[1,4,64,64]{3,2,1,0:T(8,128)(2,1)S(1)}, u32[]{:S(2)}) copy-start(bf16[1,4,64,64]{3,2,1,0:T(8,128)(2,1)S(1)} %copy.60) | copy-start | bytes 98308
  33.3 12.3 %copy-start.6 = (bf16[1,64,8192]{2,1,0:T(8,128)(2,1)S(1)}, bf16[1,64,8192]{2,1,0:T(8,128)(2,1)}, u32[]{:S(2)}) copy-start(bf16[1,64,8192]{2,1,0:T(8,128)(2,1)} %param.12) | copy-start | bytes 3145732
  36.1 14.0 %collective-permute-start.2 = (f32[64,64]{1,0:T(8,128)}, f32[64,64]{1,0:T(8,128)}, u32[]{:S(2)}, u32[]{:S(2)}) collective-permute-start(f32[64,64]{1,0:T(8,128)} %fusion.76), channel_id=1, source_target_pairs={{0,16},{16,0},{32,48},{48,32},{64,80},{80,64},{96,112},{112,96},{1... | collective-permute-start | bytes 49160 | tf_op jit(solution)/shard_map/ppermute | solution.py:35
  40.7 9.0 %copy-start.16 = (bf16[1,3,8192]{2,1,0:T(4,128)(2,1)S(1)}, bf16[1,3,8192]{2,1,0:T(4,128)(2,1)}, u32[]{:S(2)}) copy-start(bf16[1,3,8192]{2,1,0:T(4,128)(2,1)} %param.13) | copy-start | bytes 147460
  40.7 9.0 %copy-start.18 = (s32[1,63,4]{1,2,0:T(4,128)S(1)}, s32[1,63,4]{1,2,0:T(4,128)}, u32[]{:S(2)}) copy-start(s32[1,63,4]{1,2,0:T(4,128)} %param.18) | copy-start | bytes 3028
  41.2 20.0 %copy-start.19 = (s32[1,16]{1,0:T(1,128)S(1)}, s32[1,16]{1,0:T(1,128)}, u32[]{:S(2)}) copy-start(s32[1,16]{1,0:T(1,128)} %param.20) | copy-start | bytes 196
  46.4 48.8 %collective-permute-start = (bf16[67,2048]{1,0:T(8,128)(2,1)S(1)}, bf16[67,2048]{1,0:T(8,128)(2,1)S(1)}, u32[]{:S(2)}, u32[]{:S(2)}) collective-permute-start(bf16[67,2048]{1,0:T(8,128)(2,1)S(1)} %get-tuple-element.103), channel_id=1, source_target_pairs={{0,16},{16,32},{32,48},{48,64},{64,80},{80,96},{96,112},{112,128},... | collective-permute-start | bytes 823304 | tf_op jit(solution)/shard_map/ppermute | solution.py:22
  48.4 46.9 %collective-permute-start.1 = (bf16[67,2048]{1,0:T(8,128)(2,1)S(1)}, bf16[67,2048]{1,0:T(8,128)(2,1)}, u32[]{:S(2)}, u32[]{:S(2)}) collective-permute-start(bf16[67,2048]{1,0:T(8,128)(2,1)S(1)} %get-tuple-element.104), channel_id=1, source_target_pairs={{16,0},{32,16},{48,32},{64,48},{80,64},{96,80},{112,96},{128,112},... | collective-permute-start | bytes 823304 | tf_op jit(solution)/shard_map/ppermute | solution.py:23
  51.0 6.8 %collective-permute-start.3 = (f32[64,64]{1,0:T(8,128)S(1)}, f32[64,64]{1,0:T(8,128)S(1)}, u32[]{:S(2)}, u32[]{:S(2)}) collective-permute-start(f32[64,64]{1,0:T(8,128)S(1)} %fusion.64), channel_id=1, source_target_pairs={{0,32},{32,0},{16,48},{48,16},{64,96},{96,64},{80,112},{112,80},{1... | collective-permute-start | bytes 49160 | tf_op jit(solution)/shard_map/ppermute | solution.py:35
  58.0 4.9 %collective-permute-start.4 = (f32[64,64]{1,0:T(8,128)S(1)}, f32[64,64]{1,0:T(8,128)S(1)}, u32[]{:S(2)}, u32[]{:S(2)}) collective-permute-start(f32[64,64]{1,0:T(8,128)S(1)} %fusion.65), channel_id=1, source_target_pairs={{0,64},{64,0},{16,80},{80,16},{32,96},{96,32},{48,112},{112,48},{1... | collective-permute-start | bytes 49160 | tf_op jit(solution)/shard_map/ppermute | solution.py:35
  63.0 4.6 %collective-permute-start.5 = (f32[64,64]{1,0:T(8,128)S(1)}, f32[64,64]{1,0:T(8,128)S(1)}, u32[]{:S(2)}, u32[]{:S(2)}) collective-permute-start(f32[64,64]{1,0:T(8,128)S(1)} %fusion.66), channel_id=1, source_target_pairs={{0,128},{128,0},{16,144},{144,16},{32,160},{160,32},{48,176},{176,... | collective-permute-start | bytes 49160 | tf_op jit(solution)/shard_map/ppermute | solution.py:35
  404.8 5.0 %copy-start.17 = (bf16[64,64]{1,0:T(8,128)(2,1)S(1)}, bf16[64,64]{1,0:T(8,128)(2,1)}, u32[]{:S(2)}) copy-start(bf16[64,64]{1,0:T(8,128)(2,1)} %convolution_convert_fusion.3) | copy-start | bytes 24580
  404.8 6.5 %copy-start.14 = (bf16[1,8,64,64]{3,2,1,0:T(8,128)(2,1)S(1)}, bf16[1,8,64,64]{3,2,1,0:T(8,128)(2,1)}, u32[]{:S(2)}) copy-start(bf16[1,8,64,64]{3,2,1,0:T(8,128)(2,1)} %copy-done.13) | copy-start | bytes 196612
  409.8 2.2 copy-start.12
  409.8 1.8 copy-start.11
  412.0 3.1 copy-start.3
  412.0 3.1 copy-start.5
Sparse Core Ops, SparseCore 0:
  45.8 60.7 all-gather.2
where the time goes:
time: 436 us; the launch traced here: 430 us
  matrix products  212 us (49%)
  local copies, waits for them, and re-layouts  114 us (26%)
  other arithmetic  42.4 us (10%)
  blocking collectives  25.5 us (6%)
  starting transfers between devices  16.2 us (4%)
  between operations  13.9 us (3%)
  waiting for transfers between devices  5.23 us (1%)
    dot_general x24, matrix products, advance(): jnp.einsum('sib,iab->sia', picked[:rhs_count], kernel, preferred_element_...  189 us
    gather x24, local copies, waits for them, and re-layouts, advance(): picked = jnp.take(leaf_window_slice, indices + column, axis=1)  54.5 us
    all_gather x1, blocking collectives, local(): every_root = lax.all_gather(partition_root[None], 'far', axis=0, tiled=True)  25.5 us
    select_n x48, other arithmetic, advance(): picked = jnp.take(leaf_window_slice, indices + column, axis=1)  20.9 us
    and x24, other arithmetic, advance(): picked = jnp.take(leaf_window_slice, indices + column, axis=1)  16.9 us
    unnamed x51, local copies, waits for them, and re-layouts  15.3 us
    gather x2, local copies, waits for them, and re-layouts, local(): sources = jnp.take(flat_nodes, lookup.reshape(-1), axis=0)  14.4 us
    ppermute x4, starting transfers between devices, swapped(): return lax.ppermute(block, axis, route)  13 us
  transfers between devices with their start and end apart: 7, of which 3 were waited for; matrix products, arithmetic and copies ran while one was open for 70% of the time, Pallas kernels for 0%

commit v1 on v0

v1 whole, which is shorter than its diff:
```python
import functools
import math

import jax
import jax.numpy as jnp
from jax import lax
from jax.experimental import pallas as pl
from jax.experimental.pallas import tpu as pltpu
from jax.sharding import PartitionSpec as P

BF = jnp.bfloat16
F32 = jnp.float32
MESH = pl.DeviceIdType.MESH
HALO = 16
HALF_ROOT = 0.7071067811865476
SOFTEN = 0.0004
LEAVES = 64
WINDOW = LEAVES + 2 * HALO
P_SIZE = 128
RANK = 64
NEAR = 24
KC = 4
N_LEAF = 16
N_FAR = 16
PAIRS = LEAVES // 2
NODES = LEAVES - 1
BLOCKS = 32
PIECE = BLOCKS // 2
RING = N_FAR // 2
STEPS = 7
FEATS = 16
CHILD_START = (0, 64, 96, 112, 120, 124)
ROW_START = (None, 0, 32, 48, 56, 60, 62)
TOP_START = (0, 16, 24, 28)


def lanes(index, count=1):
    return pl.ds(pl.multiple_of(index * P_SIZE, P_SIZE), count * P_SIZE)


def split3(value):
    high = value.astype(BF).astype(F32)
    rest = value - high
    middle = rest.astype(BF).astype(F32)
    return high, middle, rest - middle


def stacked_rows(rows, width):
    at = lax.broadcasted_iota(jnp.int32, (FEATS, width), 0)
    out = jnp.zeros((FEATS, width), F32)
    for r, row in enumerate(rows):
        out = jnp.where(at == r, row, out)
    return out.astype(BF)


def kernel(
    offsets,
    pattern,
    root_pattern,
    coords,
    tops,
    x_hbm,
    basis_hbm,
    transfer_hbm,
    coupling_hbm,
    root_blocks_hbm,
    out_hbm,
    window,
    target_feats,
    target_turned,
    basis,
    transfer,
    coupling,
    root_blocks,
    h0,
    gathered,
    roots,
    tops_in,
    descent,
    gains,
    expansion,
    near_sum,
    out_vmem,
    load_sem,
    x_sem,
    halo_send,
    halo_recv,
    ring_send,
    ring_recv,
    sib_send,
    sib_recv,
    root_send,
    root_recv,
    top_send,
    top_recv,
):
    leaf = lax.axis_index("leaf")
    far = lax.axis_index("far")
    z = far // 2
    core = lax.rem(far, 2)
    sibling = z * 2 + (1 - core)

    def column(step):
        return lax.rem(z + RING + step, RING) * 2 + core

    def leaf_peer(k):
        return lax.rem(leaf + k + N_LEAF, N_LEAF)

    def far_peer(k):
        return lax.rem(far + k + N_FAR, N_FAR)

    barrier = pltpu.get_barrier_semaphore()
    for k in range(1, N_LEAF):
        pl.semaphore_signal(
            barrier, inc=1, device_id=(leaf_peer(k), far), device_id_type=MESH
        )
    for k in range(1, N_FAR):
        pl.semaphore_signal(
            barrier, inc=1, device_id=(leaf, far_peer(k)), device_id_type=MESH
        )

    def load_x(i):
        return pltpu.make_async_copy(
            x_hbm.at[:, lanes(i)], window.at[HALO + i, pl.ds(0, RANK)], x_sem.at[i]
        )

    def start_x(i, carry):
        load_x(i).start()
        return carry

    def wait_x(i, carry):
        load_x(i).wait()
        return carry

    lax.fori_loop(0, LEAVES, start_x, 0)
    load_basis = pltpu.make_async_copy(basis_hbm, basis, load_sem.at[1])
    load_basis.start()
    load_transfer = pltpu.make_async_copy(transfer_hbm, transfer, load_sem.at[2])
    load_transfer.start()
    load_coupling = pltpu.make_async_copy(coupling_hbm, coupling, load_sem.at[3])
    load_root_blocks = pltpu.make_async_copy(root_blocks_hbm, root_blocks, load_sem.at[4])
    load_coupling.start()
    load_root_blocks.start()

    chunk = 1024

    def make_feats(q, carry):
        at = pl.ds(pl.multiple_of(q * chunk, chunk), chunk)
        c = coords[:, at].astype(F32)
        rows = [c[r : r + 1] for r in range(3)]
        square = rows[0] * rows[0] + rows[1] * rows[1] + rows[2] * rows[2]
        one = jnp.ones_like(square)
        feats = stacked_rows([*rows, one, one, one, *split3(square)], chunk)
        for t in range(chunk // P_SIZE):
            window[HALO + q * (chunk // P_SIZE) + t, RANK : RANK + FEATS] = feats[
                :, t * P_SIZE : (t + 1) * P_SIZE
            ]
        target_feats[:, at] = stacked_rows(
            [*(-2.0 * row for row in rows), *split3(square + SOFTEN), one, one, one], chunk
        )
        return carry

    lax.fori_loop(0, LEAVES * P_SIZE // chunk, make_feats, 0)
    lax.fori_loop(0, LEAVES, wait_x, 0)
    pl.semaphore_wait(barrier, N_LEAF - 1 + N_FAR - 1)

    halo = []
    for way, (src, dst) in enumerate(((LEAVES, 0), (HALO, LEAVES + HALO))):
        copy = pltpu.make_async_remote_copy(
            src_ref=window.at[pl.ds(src, HALO)],
            dst_ref=window.at[pl.ds(dst, HALO)],
            send_sem=halo_send.at[way],
            recv_sem=halo_recv.at[way],
            device_id=(leaf_peer(1 if way == 0 else -1), far),
            device_id_type=MESH,
        )
        copy.start()
        halo.append(copy)

    load_basis.wait()

    def leaf_pair(q, carry):
        parts = []
        for t in range(2):
            x = window[HALO + 2 * q + t, 0:RANK]
            b = basis[:, lanes(2 * q + t)]
            parts.append(
                lax.dot_general(
                    x, b, (((1,), (1,)), ((), ())), preferred_element_type=F32
                )
            )
        h0[q] = jnp.concatenate(parts, axis=1).astype(BF)
        return carry

    lax.fori_loop(0, PAIRS, leaf_pair, 0, unroll=8)
    load_transfer.wait()

    def piece_of(way, step):
        return 1 - lax.rem(step, 2) if way == 1 else lax.rem(step, 2)

    def ring_copy(way, step):
        piece = piece_of(way, step)
        behind = step // 2
        block = gathered.at[
            column(-behind if way == 0 else behind), pl.ds(piece * PIECE, PIECE)
        ]
        return pltpu.make_async_remote_copy(
            src_ref=block,
            dst_ref=block,
            send_sem=ring_send.at[way, step],
            recv_sem=ring_recv.at[way, step],
            device_id=(leaf, column(1 if way == 0 else -1)),
            device_id_type=MESH,
        )

    def sib_copy(way, step):
        piece = piece_of(way, step)
        behind = step // 2 + 1
        part = far if way == 2 else column(-behind if way == 0 else behind)
        block = gathered.at[part, pl.ds(piece * PIECE, PIECE)]
        return pltpu.make_async_remote_copy(
            src_ref=block,
            dst_ref=block,
            send_sem=sib_send.at[way, step],
            recv_sem=sib_recv.at[way, step],
            device_id=(leaf, sibling),
            device_id_type=MESH,
        )

    def up_node(source, first_child, j):
        e = transfer[pl.ds(first_child + 2 * j, 2)].reshape(2 * RANK, RANK)
        return jnp.dot(source[j], e, preferred_element_type=F32) * HALF_ROOT

    def up_level(level, source, first_block):
        first_child = CHILD_START[level - 1]

        def pair(q, carry):
            both = [up_node(source, first_child, 2 * q + t) for t in range(2)]
            gathered[far, first_block + q] = jnp.concatenate(both, axis=1).astype(BF)
            return carry

        count = LEAVES >> (level + 1)
        lax.fori_loop(0, count, pair, 0, unroll=min(count, 8))

    mine = gathered.at[far]
    up_level(1, h0, 0)
    ring_copy(0, 0).start()
    ring_copy(1, 1).start()
    sib_copy(2, 0).start()
    for level in range(2, 6):
        up_level(
            level,
            mine.at[pl.ds(ROW_START[level - 1] // 2, LEAVES >> level)],
            ROW_START[level] // 2,
        )
    root = up_node(mine.at[pl.ds(ROW_START[5] // 2, 1)], CHILD_START[5], 0).astype(BF)
    root = jnp.concatenate([root, jnp.zeros_like(root)], axis=1)
    gathered[far, BLOCKS - 1] = root
    roots[leaf] = root
    ring_copy(0, 1).start()
    ring_copy(1, 0).start()
    root_copies = []
    for k in range(1, N_LEAF):
        copy = pltpu.make_async_remote_copy(
            src_ref=gathered.at[far, BLOCKS - 1],
            dst_ref=roots.at[leaf],
            send_sem=root_send.at[k],
            recv_sem=root_recv.at[k],
            device_id=(leaf_peer(k), far),
            device_id_type=MESH,
        )
        copy.start()
        root_copies.append(copy)
    sib_copy(2, 1).start()

    for copy in halo:
        copy.wait()

    blank_row = lax.broadcasted_iota(jnp.int32, (FEATS, P_SIZE), 0)
    blank = jnp.where((blank_row >= 3) & (blank_row < 6), 1.0, 0.0).astype(BF)
    for where, first in ((0, 0), (N_LEAF - 1, LEAVES + HALO)):

        @pl.when(leaf == where)
        def _():
            for t in range(HALO):
                window[first + t, 0:RANK] = jnp.zeros((RANK, P_SIZE), BF)
                window[first + t, RANK : RANK + FEATS] = blank

    def turn(q, carry):
        block = jnp.concatenate(
            [target_feats[:, lanes(8 * q + t)] for t in range(8)], axis=0
        )
        block = block.astype(F32).T.astype(BF)
        for t in range(8):
            target_turned[8 * q + t] = block[:, t * FEATS : (t + 1) * FEATS]
        return carry

    lax.fori_loop(0, LEAVES // 8, turn, 0)

    def top_up():
        for copy in root_copies:
            copy.wait()
        h = [roots[g][:, :RANK] for g in range(N_LEAF)]
        for level in range(4):
            start = TOP_START[level]
            mapped = [
                jnp.dot(h[g], tops[start + g], preferred_element_type=F32)
                for g in range(len(h))
            ]
            h = [
                ((mapped[2 * g] + mapped[2 * g + 1]) * HALF_ROOT).astype(BF)
                for g in range(len(h) // 2)
            ]
        tops_in[far] = jnp.concatenate([h[0], h[0]], axis=1)

    def top_copy(k):
        block = tops_in.at[far]
        return pltpu.make_async_remote_copy(
            src_ref=block,
            dst_ref=block,
            send_sem=top_send.at[k],
            recv_sem=top_recv.at[k],
            device_id=(leaf, far_peer(k)),
            device_id_type=MESH,
        )

    def top_down():
        for k in range(1, N_FAR):
            top_copy(k).wait()
        load_root_blocks.wait()
        local = jnp.zeros((RANK, RANK), F32)
        for p in range(N_FAR):
            local = local + root_pattern[0, p].astype(F32) * jnp.dot(
                tops_in[p][:, :RANK], root_blocks[p], preferred_element_type=F32
            )
        for level in reversed(range(4)):
            e = tops[TOP_START[level] + lax.shift_right_logical(leaf, level)]
            local = lax.dot_general(
                local.astype(BF), e, (((1,), (1,)), ((), ())), preferred_element_type=F32
            )
        descent[...] = local

    def near_leaf(i, carry):
        target = target_turned[i]
        total = jnp.zeros((RANK, P_SIZE), F32)
        for q in range(NEAR // 2):
            near = [offsets[i, 2 * q + t] + (i + HALO) for t in range(2)]
            source = jnp.concatenate(
                [window[at, RANK : RANK + FEATS] for at in near], axis=1
            )
            x = jnp.concatenate([window[at, 0:RANK] for at in near], axis=1)
            inverse = lax.rsqrt(
                jnp.dot(target, source, preferred_element_type=F32).astype(BF)
            )
            total = total + lax.dot_general(
                x, inverse, (((1,), (1,)), ((), ())), preferred_element_type=F32
            )
        near_sum[:, lanes(i)] = total
        return carry

    def segment(step, carry):
        lax.fori_loop(
            step * LEAVES // STEPS, (step + 1) * LEAVES // STEPS, near_leaf, 0
        )
        for way in range(2):
            ring_copy(way, step).wait_recv()

            @pl.when(step + 2 < STEPS)
            def _():
                ring_copy(way, step + 2).start()

            sib_copy(way, step).start()

        @pl.when(step == 0)
        def _():
            top_up()
            for k in range(1, N_FAR):
                top_copy(k).start()

        @pl.when(step == 2)
        def _():
            top_down()

        return carry

    lax.fori_loop(0, STEPS, segment, 0)

    for step in range(STEPS):
        for way in range(2):
            ring_copy(way, step).wait_send()
            sib_copy(way, step).wait()
    for piece in range(2):
        sib_copy(2, piece).wait()
    load_coupling.wait()

    def gain(row, parity):
        block = row // 2
        parts = [
            gathered[pattern[row, k], block][:, parity * RANK : (parity + 1) * RANK]
            for k in range(KC)
        ]
        gains[row] = jnp.dot(
            jnp.concatenate(parts, axis=1),
            coupling[row].reshape(KC * RANK, RANK),
            preferred_element_type=F32,
        )

    def gain_pair(q, carry):
        gain(2 * q, 0)
        gain(2 * q + 1, 1)
        return carry

    lax.fori_loop(0, NODES // 2, gain_pair, 0, unroll=4)
    gain(NODES - 1, 0)

    def down(level, j):
        start = CHILD_START[level - 1]
        e = transfer[pl.ds(start + 2 * j, 2)].reshape(2 * RANK, RANK)
        return lax.dot_general(
            expansion[ROW_START[level] + j],
            e,
            (((1,), (1,)), ((), ())),
            preferred_element_type=F32,
        )

    expansion[NODES - 1] = (descent[...] + gains[NODES - 1]).astype(BF)

    def down_level(level):
        def node(j, carry):
            both = down(level, j)
            for t in range(2):
                row = ROW_START[level - 1] + 2 * j + t
                expansion[row] = (
                    both[:, t * RANK : (t + 1) * RANK] + gains[row]
                ).astype(BF)
            return carry

        count = LEAVES >> level
        lax.fori_loop(0, count, node, 0, unroll=min(count, 8))

    for level in range(6, 1, -1):
        down_level(level)

    factor = 1.0 / math.sqrt(NEAR * P_SIZE)

    def finish(j, carry):
        both = down(1, j).astype(BF)
        for t in range(2):
            at = lanes(2 * j + t)
            far_sum = jnp.dot(
                both[:, t * RANK : (t + 1) * RANK], basis[:, at], preferred_element_type=F32
            )
            out_vmem[:, at] = (near_sum[:, at] * factor + far_sum).astype(BF)
        return carry

    lax.fori_loop(0, PAIRS, finish, 0, unroll=4)
    store = pltpu.make_async_copy(out_vmem, out_hbm, load_sem.at[0])
    store.start()
    store.wait()


def local(
    right_sides,
    point_coords,
    near_offsets,
    leaf_basis,
    local_transfer,
    top_transfer,
    coupling_pattern,
    coupling_blocks,
    root_pattern,
    root_blocks,
):
    smem = pl.BlockSpec(memory_space=pltpu.SMEM)
    vmem = pl.BlockSpec(memory_space=pltpu.VMEM)
    hbm = pl.BlockSpec(memory_space=pl.ANY)
    points = LEAVES * P_SIZE
    dma = pltpu.SemaphoreType.DMA
    out = pl.pallas_call(
        kernel,
        name="h2_product",
        out_shape=jax.ShapeDtypeStruct((RANK, points), BF),
        in_specs=[smem, smem, smem, vmem, vmem, hbm, hbm, hbm, hbm, hbm],
        out_specs=hbm,
        scratch_shapes=[
            pltpu.VMEM((WINDOW, RANK + FEATS, P_SIZE), BF),
            pltpu.VMEM((FEATS, points), BF),
            pltpu.VMEM((LEAVES, P_SIZE, FEATS), BF),
            pltpu.VMEM((RANK, points), BF),
            pltpu.VMEM((2 * NODES, RANK, RANK), BF),
            pltpu.VMEM((NODES, KC, RANK, RANK), BF),
            pltpu.VMEM((N_FAR, RANK, RANK), BF),
            pltpu.VMEM((PAIRS, RANK, 2 * RANK), BF),
            pltpu.VMEM((N_FAR, BLOCKS, RANK, 2 * RANK), BF),
            pltpu.VMEM((N_LEAF, RANK, 2 * RANK), BF),
            pltpu.VMEM((N_FAR, RANK, 2 * RANK), BF),
            pltpu.VMEM((RANK, RANK), F32),
            pltpu.VMEM((NODES, RANK, RANK), F32),
            pltpu.VMEM((NODES, RANK, RANK), BF),
            pltpu.VMEM((RANK, points), F32),
            pltpu.VMEM((RANK, points), BF),
            dma((5,)),
            dma((LEAVES,)),
            dma((2,)),
            dma((2,)),
            dma((2, STEPS)),
            dma((2, STEPS)),
            dma((3, STEPS)),
            dma((3, STEPS)),
            dma((N_LEAF,)),
            dma((N_LEAF,)),
            dma((N_FAR,)),
            dma((N_FAR,)),
        ],
        compiler_params=pltpu.CompilerParams(
            collective_id=0, has_side_effects=True, vmem_limit_bytes=52 << 20
        ),
        cost_estimate=pl.CostEstimate(
            flops=4 << 30, bytes_accessed=16 << 20, transcendentals=25 << 20
        ),
    )(
        near_offsets[0],
        coupling_pattern[0],
        root_pattern,
        point_coords[0],
        top_transfer[0],
        right_sides[0],
        leaf_basis[0],
        local_transfer[0],
        coupling_blocks[0],
        root_blocks[0],
    )
    return out[None]


def solution(mesh):
    return jax.shard_map(
        local,
        mesh=mesh,
        in_specs=(
            P("far", None, "leaf"),
            P("far", None, "leaf"),
            P("far", "leaf", None),
            P("far", None, "leaf"),
            P("far", "leaf", None, None),
            P("far", None, None, None),
            P("far", "leaf", None),
            P("far", "leaf", None, None, None),
            P("far", None),
            P("far", None, None, None),
        ),
        out_specs=P("far", None, "leaf"),
        check_vma=False,
    )
```

time: 436 us -> 112 us (0.26); the launches traced: 430 us -> 111 us
  matrix products: 212 us -> 0 us
  local copies, waits for them, and re-layouts: 114 us -> 10.9 us
  Pallas kernels: 0 us -> 100 us
  other arithmetic: 42.4 us -> 0 us
  blocking collectives: 25.5 us -> 0 us
  starting transfers between devices: 16.2 us -> 0 us
  between operations: 13.9 us -> 0.01 us
  waiting for transfers between devices: 5.23 us -> 0 us
    dot_general x44 -> x0, matrix products: 212 us -> none  [the longest x24 189 us: advance(): jnp.einsum('sib,iab->sia', picked[:rhs_count], kernel, preferred_element_...]
    pallas_call x0 -> x1, Pallas kernels: none -> 100 us  [local(): pl.pallas_call(kernel, name='h2_product', out_shape=jax.ShapeDtypeStruct(...]
    gather x26 -> x0, local copies, waits for them, and re-layouts: 68.9 us -> none  [the longest x24 54.5 us: advance(): picked = jnp.take(leaf_window_slice, indices + column, axis=1)]
    all_gather x1 -> x0, blocking collectives: 25.5 us -> none  [local(): every_root = lax.all_gather(partition_root[None], 'far', axis=0, tiled=True)]
    select_n x49 -> x0, other arithmetic: 20.9 us -> none  [the longest x48 20.9 us: advance(): picked = jnp.take(leaf_window_slice, indices + column, axis=1)]
    and x25 -> x0, other arithmetic: 16.9 us -> none  [the longest x24 16.9 us: advance(): picked = jnp.take(leaf_window_slice, indices + column, axis=1)]
    ppermute x6 -> x0, starting transfers between devices: 16.2 us -> none  [the longest x4 13 us: swapped(): return lax.ppermute(block, axis, route)]
    slice x29 -> x0, local copies, waits for them, and re-layouts: 9.93 us -> none  [the longest x5 8.25 us: local(): transfer[first_child:first_child + width_now]]
  transfers between devices with their start and end apart: 7 -> 0, of which waited for: 3 -> 0; matrix products, arithmetic and copies ran while one was open for 70% -> 0% of each run, Pallas kernels for 0% -> 0%
where the time goes in v1:
time: 112 us; the launch traced here: 111 us
  Pallas kernels  100 us (89%)
  local copies, waits for them, and re-layouts  10.9 us (10%)
    pallas_call x1, Pallas kernels, local(): pl.pallas_call(kernel, name='h2_product', out_shape=jax.ShapeDtypeStruct(...  100 us
    unnamed x12, local copies, waits for them, and re-layouts  10.9 us

profile of v1, /device:TPU:1, one launch (start us, length us, event | category | flops | bytes accessed | tf_op | source)
XLA Modules:
  0.0 111.4 jit_solution(10938430691457574032)
XLA Ops:
  0.0 0.8 copy.11
  0.8 0.8 copy.12
  1.6 4.9 %copy.13 = bf16[1,126,64,64]{3,2,1,0:T(8,128)(2,1)} copy(bf16[1,126,64,64]{1,3,2,0:T(8,128)(2,1)} %param.14) | data formatting | bytes 2064384 | tf_op args[4]
  6.5 0.0 copy-start
  6.5 1.0 copy-done
  7.5 0.0 copy-start.1
  7.5 0.9 copy-done.1
  8.5 0.0 copy-start.2
  8.5 0.8 copy-done.2
  9.3 0.0 copy-start.3
  9.3 0.7 copy-done.3
  10.0 100.4 %h2_product.1 = bf16[64,8192]{1,0:T(8,128)(2,1)S(1)} custom-call(s32[64,24]{1,0:T(8,128)S(1)} %bitcast.11, s32[63,4]{1,0:T(8,128)S(1)} %bitcast.12, s32[1,16]{1,0:T(1,128)S(1)} %copy-done.3, bf16[3,8192]{1,0:T(4,128)(2,1)S(1)} %bitcast.15, bf16[30,64,64]{2,1,0:T(8,128)(2,1)S(1)} %bitcast.13, bf16[64,8192]{1,0:T(8,128)(2,1)} %bitcast.18, ...), custom_call_target="tpu_custom_call" | custom-call | flops 4294967296 | bytes 16777216 | tf_op jit(solution)/shard_map/h2_product/pallas_call | solution.py:479
  110.4 1.0 copy.15
Async XLA Ops:
  6.5 1.0 copy-start
  7.5 0.9 copy-start.1
  8.5 0.8 copy-start.2
  9.3 0.7 copy-start.3

commit v2 on v1

--- a/solution.py
+++ b/solution.py
@@ -28,6 +28,8 @@
 PIECE = BLOCKS // 2
 RING = N_FAR // 2
 STEPS = 7
+GROUP = 4
+GROUPS = LEAVES // GROUP
 FEATS = 16
 CHILD_START = (0, 64, 96, 112, 120, 124)
 ROW_START = (None, 0, 32, 48, 56, 60, 62)
@@ -43,6 +45,14 @@
     rest = value - high
     middle = rest.astype(BF).astype(F32)
     return high, middle, rest - middle
+
+
+def folded(square):
+    return jnp.concatenate([square[: RANK // 2], square[RANK // 2 :]], axis=1)
+
+
+def unfolded(block):
+    return jnp.concatenate([block[:, :RANK], block[:, RANK:]], axis=0)
 
 
 def stacked_rows(rows, width):
@@ -67,7 +77,8 @@
     out_hbm,
     window,
     target_feats,
-    target_turned,
+    halo_in,
+    source_coords,
     basis,
     transfer,
     coupling,
@@ -77,7 +88,6 @@
     roots,
     tops_in,
     descent,
-    gains,
     expansion,
     near_sum,
     out_vmem,
@@ -165,10 +175,10 @@
     pl.semaphore_wait(barrier, N_LEAF - 1 + N_FAR - 1)
 
     halo = []
-    for way, (src, dst) in enumerate(((LEAVES, 0), (HALO, LEAVES + HALO))):
+    for way, src in enumerate((LEAVES, HALO)):
         copy = pltpu.make_async_remote_copy(
             src_ref=window.at[pl.ds(src, HALO)],
-            dst_ref=window.at[pl.ds(dst, HALO)],
+            dst_ref=halo_in.at[way],
             send_sem=halo_send.at[way],
             recv_sem=halo_recv.at[way],
             device_id=(leaf_peer(1 if way == 0 else -1), far),
@@ -227,42 +237,38 @@
             device_id_type=MESH,
         )
 
-    def up_node(source, first_child, j):
-        e = transfer[pl.ds(first_child + 2 * j, 2)].reshape(2 * RANK, RANK)
-        return jnp.dot(source[j], e, preferred_element_type=F32) * HALF_ROOT
-
-    def up_level(level, source, first_block):
-        first_child = CHILD_START[level - 1]
-
-        def pair(q, carry):
-            both = [up_node(source, first_child, 2 * q + t) for t in range(2)]
-            gathered[far, first_block + q] = jnp.concatenate(both, axis=1).astype(BF)
-            return carry
-
-        count = LEAVES >> (level + 1)
-        lax.fori_loop(0, count, pair, 0, unroll=min(count, 8))
-
-    mine = gathered.at[far]
-    up_level(1, h0, 0)
+    def up_level(level, sources):
+        values = []
+        for j, source in enumerate(sources):
+            first = CHILD_START[level - 1] + 2 * j
+            e = transfer[pl.ds(first, 2)].reshape(2 * RANK, RANK)
+            values.append(jnp.dot(source, e, preferred_element_type=F32) * HALF_ROOT)
+        return [
+            jnp.concatenate(values[2 * q : 2 * q + 2], axis=1).astype(BF)
+            for q in range(len(values) // 2)
+        ]
+
+    level1 = up_level(1, [h0[j] for j in range(PAIRS)])
+    for q, block in enumerate(level1):
+        gathered[far, q] = block
     ring_copy(0, 0).start()
     ring_copy(1, 1).start()
     sib_copy(2, 0).start()
+    blocks = level1
     for level in range(2, 6):
-        up_level(
-            level,
-            mine.at[pl.ds(ROW_START[level - 1] // 2, LEAVES >> level)],
-            ROW_START[level] // 2,
-        )
-    root = up_node(mine.at[pl.ds(ROW_START[5] // 2, 1)], CHILD_START[5], 0).astype(BF)
-    root = jnp.concatenate([root, jnp.zeros_like(root)], axis=1)
-    gathered[far, BLOCKS - 1] = root
-    roots[leaf] = root
+        blocks = up_level(level, blocks)
+        for q, block in enumerate(blocks):
+            gathered[far, ROW_START[level] // 2 + q] = block
+    e = transfer[pl.ds(CHILD_START[5], 2)].reshape(2 * RANK, RANK)
+    root = (jnp.dot(blocks[0], e, preferred_element_type=F32) * HALF_ROOT).astype(BF)
+    gathered[far, BLOCKS - 1] = jnp.concatenate([root, jnp.zeros_like(root)], axis=1)
+    roots[leaf] = folded(root)
     ring_copy(0, 1).start()
     ring_copy(1, 0).start()
     root_copies = []
     for k in range(1, N_LEAF):
         copy = pltpu.make_async_remote_copy(
-            src_ref=gathered.at[far, BLOCKS - 1],
+            src_ref=roots.at[leaf],
             dst_ref=roots.at[leaf],
             send_sem=root_send.at[k],
             recv_sem=root_recv.at[k],
@@ -273,34 +279,45 @@
         root_copies.append(copy)
     sib_copy(2, 1).start()
 
-    for copy in halo:
-        copy.wait()
-
-    blank_row = lax.broadcasted_iota(jnp.int32, (FEATS, P_SIZE), 0)
-    blank = jnp.where((blank_row >= 3) & (blank_row < 6), 1.0, 0.0).astype(BF)
-    for where, first in ((0, 0), (N_LEAF - 1, LEAVES + HALO)):
-
-        @pl.when(leaf == where)
-        def _():
-            for t in range(HALO):
-                window[first + t, 0:RANK] = jnp.zeros((RANK, P_SIZE), BF)
-                window[first + t, RANK : RANK + FEATS] = blank
-
-    def turn(q, carry):
+    def spread(q, carry):
         block = jnp.concatenate(
-            [target_feats[:, lanes(8 * q + t)] for t in range(8)], axis=0
-        )
-        block = block.astype(F32).T.astype(BF)
+            [window[8 * q + t, RANK : RANK + FEATS] for t in range(8)], axis=0
+        )
+        block = block.astype(F32).T
         for t in range(8):
-            target_turned[8 * q + t] = block[:, t * FEATS : (t + 1) * FEATS]
-        return carry
-
-    lax.fori_loop(0, LEAVES // 8, turn, 0)
+            for c in range(3):
+                at = t * FEATS + c
+                source_coords[8 * q + t, c] = jnp.broadcast_to(
+                    block[:, at : at + 1], (P_SIZE, P_SIZE)
+                )
+        return carry
+
+    lax.fori_loop(HALO // 8, (HALO + LEAVES) // 8, spread, 0)
+
+    def halo_arrived():
+        for copy in halo:
+            copy.wait()
+        row = lax.broadcasted_iota(jnp.int32, (RANK + FEATS, P_SIZE), 0)
+        blank = jnp.where((row >= RANK + 3) & (row < RANK + 6), 1.0, 0.0).astype(BF)
+        for way, (edge, first) in enumerate(((0, 0), (N_LEAF - 1, HALO + LEAVES))):
+
+            @pl.when(leaf == edge)
+            def _():
+                for t in range(HALO):
+                    window[first + t] = blank
+
+            @pl.when(leaf != edge)
+            def _():
+                for t in range(HALO):
+                    window[first + t] = halo_in[way, t]
+
+            lax.fori_loop(first // 8, (first + HALO) // 8, spread, 0)
+
 
     def top_up():
         for copy in root_copies:
             copy.wait()
-        h = [roots[g][:, :RANK] for g in range(N_LEAF)]
+        h = [unfolded(roots[g]) for g in range(N_LEAF)]
         for level in range(4):
             start = TOP_START[level]
             mapped = [
@@ -311,7 +328,7 @@
                 ((mapped[2 * g] + mapped[2 * g + 1]) * HALF_ROOT).astype(BF)
                 for g in range(len(h) // 2)
             ]
-        tops_in[far] = jnp.concatenate([h[0], h[0]], axis=1)
+        tops_in[far] = folded(h[0])
 
     def top_copy(k):
         block = tops_in.at[far]
@@ -331,7 +348,7 @@
         local = jnp.zeros((RANK, RANK), F32)
         for p in range(N_FAR):
             local = local + root_pattern[0, p].astype(F32) * jnp.dot(
-                tops_in[p][:, :RANK], root_blocks[p], preferred_element_type=F32
+                unfolded(tops_in[p]), root_blocks[p], preferred_element_type=F32
             )
         for level in reversed(range(4)):
             e = tops[TOP_START[level] + lax.shift_right_logical(leaf, level)]
@@ -340,27 +357,49 @@
             )
         descent[...] = local
 
-    def near_leaf(i, carry):
-        target = target_turned[i]
+    def near_leaf(i):
+        target = target_feats[:, lanes(i)].astype(F32).T.astype(BF)
+        c = coords[:, lanes(i)].astype(F32)
+        own = [
+            jnp.broadcast_to(c[r : r + 1], (P_SIZE, P_SIZE)).astype(BF) for r in range(3)
+        ]
         total = jnp.zeros((RANK, P_SIZE), F32)
         for q in range(NEAR // 2):
-            near = [offsets[i, 2 * q + t] + (i + HALO) for t in range(2)]
-            source = jnp.concatenate(
-                [window[at, RANK : RANK + FEATS] for at in near], axis=1
-            )
+            near = [offsets[2 * q + t, i] + (i + HALO) for t in range(2)]
             x = jnp.concatenate([window[at, 0:RANK] for at in near], axis=1)
-            inverse = lax.rsqrt(
-                jnp.dot(target, source, preferred_element_type=F32).astype(BF)
-            )
-            total = total + lax.dot_general(
-                x, inverse, (((1,), (1,)), ((), ())), preferred_element_type=F32
-            )
-        near_sum[:, lanes(i)] = total
+            if q % 3 == 0:
+                source = jnp.concatenate(
+                    [window[at, RANK : RANK + FEATS] for at in near], axis=1
+                )
+                square = jnp.dot(target, source, preferred_element_type=F32)
+                total = total + lax.dot_general(
+                    x,
+                    lax.rsqrt(square.astype(BF)),
+                    (((1,), (1,)), ((), ())),
+                    preferred_element_type=F32,
+                )
+            else:
+                inverse = []
+                for at in near:
+                    d = [source_coords[at, r].astype(BF) - own[r] for r in range(3)]
+                    square = d[0] * d[0] + jnp.asarray(SOFTEN, BF)
+                    square = square + d[1] * d[1]
+                    square = square + d[2] * d[2]
+                    inverse.append(lax.rsqrt(square))
+                total = total + jnp.dot(
+                    x, jnp.concatenate(inverse, axis=0), preferred_element_type=F32
+                )
+        return total
+
+    def near_group(step, carry):
+        p = lax.rem(step + HALO // GROUP, GROUPS)
+        for t in range(GROUP):
+            near_sum[:, lanes(GROUP * p + t)] = near_leaf(GROUP * p + t)
         return carry
 
     def segment(step, carry):
         lax.fori_loop(
-            step * LEAVES // STEPS, (step + 1) * LEAVES // STEPS, near_leaf, 0
+            step * GROUPS // STEPS, (step + 1) * GROUPS // STEPS, near_group, 0
         )
         for way in range(2):
             ring_copy(way, step).wait_recv()
@@ -378,6 +417,10 @@
                 top_copy(k).start()
 
         @pl.when(step == 2)
+        def _():
+            halo_arrived()
+
+        @pl.when(step == 3)
         def _():
             top_down()
 
@@ -393,67 +436,48 @@
         sib_copy(2, piece).wait()
     load_coupling.wait()
 
-    def gain(row, parity):
-        block = row // 2
-        parts = [
-            gathered[pattern[row, k], block][:, parity * RANK : (parity + 1) * RANK]
-            for k in range(KC)
-        ]
-        gains[row] = jnp.dot(
+    def gain(row):
+        half = slice((row % 2) * RANK, (row % 2 + 1) * RANK)
+        parts = [gathered[pattern[k, row], row // 2][:, half] for k in range(KC)]
+        return jnp.dot(
             jnp.concatenate(parts, axis=1),
             coupling[row].reshape(KC * RANK, RANK),
             preferred_element_type=F32,
         )
 
-    def gain_pair(q, carry):
-        gain(2 * q, 0)
-        gain(2 * q + 1, 1)
-        return carry
-
-    lax.fori_loop(0, NODES // 2, gain_pair, 0, unroll=4)
-    gain(NODES - 1, 0)
-
-    def down(level, j):
+    def down(level, j, value):
         start = CHILD_START[level - 1]
         e = transfer[pl.ds(start + 2 * j, 2)].reshape(2 * RANK, RANK)
-        return lax.dot_general(
-            expansion[ROW_START[level] + j],
-            e,
-            (((1,), (1,)), ((), ())),
-            preferred_element_type=F32,
-        )
-
-    expansion[NODES - 1] = (descent[...] + gains[NODES - 1]).astype(BF)
-
-    def down_level(level):
-        def node(j, carry):
-            both = down(level, j)
-            for t in range(2):
-                row = ROW_START[level - 1] + 2 * j + t
-                expansion[row] = (
-                    both[:, t * RANK : (t + 1) * RANK] + gains[row]
-                ).astype(BF)
-            return carry
-
-        count = LEAVES >> level
-        lax.fori_loop(0, count, node, 0, unroll=min(count, 8))
-
+        both = lax.dot_general(
+            value, e, (((1,), (1,)), ((), ())), preferred_element_type=F32
+        )
+        return both[:, :RANK], both[:, RANK:]
+
+    values = [(descent[...] + gain(NODES - 1)).astype(BF)]
     for level in range(6, 1, -1):
-        down_level(level)
+        children = []
+        for j, value in enumerate(values):
+            children += down(level, j, value)
+        values = [
+            (child + gain(ROW_START[level - 1] + j)).astype(BF)
+            for j, child in enumerate(children)
+        ]
+    for j, value in enumerate(values):
+        expansion[j] = value
 
     factor = 1.0 / math.sqrt(NEAR * P_SIZE)
 
     def finish(j, carry):
-        both = down(1, j).astype(BF)
+        both = down(1, j, expansion[j])
         for t in range(2):
             at = lanes(2 * j + t)
             far_sum = jnp.dot(
-                both[:, t * RANK : (t + 1) * RANK], basis[:, at], preferred_element_type=F32
+                both[t].astype(BF), basis[:, at], preferred_element_type=F32
             )
             out_vmem[:, at] = (near_sum[:, at] * factor + far_sum).astype(BF)
         return carry
 
-    lax.fori_loop(0, PAIRS, finish, 0, unroll=4)
+    lax.fori_loop(0, PAIRS, finish, 0, unroll=8)
     store = pltpu.make_async_copy(out_vmem, out_hbm, load_sem.at[0])
     store.start()
     store.wait()
@@ -485,18 +509,18 @@
         scratch_shapes=[
             pltpu.VMEM((WINDOW, RANK + FEATS, P_SIZE), BF),
             pltpu.VMEM((FEATS, points), BF),
-            pltpu.VMEM((LEAVES, P_SIZE, FEATS), BF),
+            pltpu.VMEM((2, HALO, RANK + FEATS, P_SIZE), BF),
+            pltpu.VMEM((WINDOW, 3, P_SIZE, P_SIZE), F32),
             pltpu.VMEM((RANK, points), BF),
             pltpu.VMEM((2 * NODES, RANK, RANK), BF),
             pltpu.VMEM((NODES, KC, RANK, RANK), BF),
             pltpu.VMEM((N_FAR, RANK, RANK), BF),
             pltpu.VMEM((PAIRS, RANK, 2 * RANK), BF),
             pltpu.VMEM((N_FAR, BLOCKS, RANK, 2 * RANK), BF),
-            pltpu.VMEM((N_LEAF, RANK, 2 * RANK), BF),
-            pltpu.VMEM((N_FAR, RANK, 2 * RANK), BF),
+            pltpu.VMEM((N_LEAF, RANK // 2, 2 * RANK), BF),
+            pltpu.VMEM((N_FAR, RANK // 2, 2 * RANK), BF),
             pltpu.VMEM((RANK, RANK), F32),
-            pltpu.VMEM((NODES, RANK, RANK), F32),
-            pltpu.VMEM((NODES, RANK, RANK), BF),
+            pltpu.VMEM((PAIRS, RANK, RANK), BF),
             pltpu.VMEM((RANK, points), F32),
             pltpu.VMEM((RANK, points), BF),
             dma((5,)),
@@ -513,14 +537,14 @@
             dma((N_FAR,)),
         ],
         compiler_params=pltpu.CompilerParams(
-            collective_id=0, has_side_effects=True, vmem_limit_bytes=52 << 20
+            collective_id=0, has_side_effects=True, vmem_limit_bytes=62 << 20
         ),
         cost_estimate=pl.CostEstimate(
             flops=4 << 30, bytes_accessed=16 << 20, transcendentals=25 << 20
         ),
     )(
-        near_offsets[0],
-        coupling_pattern[0],
+        near_offsets[0].T,
+        coupling_pattern[0].T,
         root_pattern,
         point_coords[0],
         top_transfer[0],

time: 112 us -> 80.5 us (0.72)
  Pallas kernels: 100 us -> 73.2 us
  local copies, waits for them, and re-layouts: 10.9 us -> 7.18 us
    pallas_call x1, Pallas kernels: 100 us -> 73.2 us  [local(): pl.pallas_call(kernel, name='h2_product', out_shape=jax.ShapeDtypeStruct(...]
    unnamed x12 -> x2, local copies, waits for them, and re-layouts: 10.9 us -> 7.18 us
where the time goes in v2:
time: 80.5 us; the launch traced here: 80.4 us
  Pallas kernels  73.2 us (91%)
  local copies, waits for them, and re-layouts  7.18 us (9%)
    pallas_call x1, Pallas kernels, local(): pl.pallas_call(kernel, name='h2_product', out_shape=jax.ShapeDtypeStruct(...  73.2 us
    unnamed x2, local copies, waits for them, and re-layouts  7.18 us

profile of v2, /device:TPU:1, one launch (start us, length us, event | category | flops | bytes accessed | tf_op | source)
XLA Modules:
  0.0 80.4 jit_solution(6088123955257067798)
XLA Ops:
  0.0 4.9 %copy.11 = bf16[1,126,64,64]{3,2,1,0:T(8,128)(2,1)} copy(bf16[1,126,64,64]{1,3,2,0:T(8,128)(2,1)} %param.14) | data formatting | bytes 2064384 | tf_op args[4]
  4.9 73.2 %h2_product.1 = bf16[64,8192]{1,0:T(8,128)(2,1)} custom-call(s32[24,64]{1,0:T(8,128)} %bitcast.22, s32[4,63]{1,0:T(4,128)} %bitcast.23, s32[1,16]{1,0:T(1,128)} %root_pattern.1, bf16[3,8192]{1,0:T(4,128)(2,1)} %bitcast.21, bf16[30,64,64]{2,1,0:T(8,128)(2,1)} %bitcast.19, bf16[64,8192]{1,0:T(8,128)(2,1)} %bitcast.17, bf16[64,8192]{1,0:T(8,128)(2,1)} %bitcast.18, ...), custom_call_target="tpu_custom_call" | custom-call | flops 4294967296 | bytes 16777216 | tf_op jit(solution)/shard_map/h2_product/pallas_call | solution.py:503
  78.1 2.3 %copy.13 = bf16[1,64,8192]{2,1,0:T(8,128)(2,1)} copy(bf16[1,64,8192]{2,1,0:T(8,128)(2,1)} %bitcast.15) | data formatting | bytes 2097152

commit v3 on v2

--- a/solution.py
+++ b/solution.py
@@ -24,13 +24,27 @@
 N_FAR = 16
 PAIRS = LEAVES // 2
 NODES = LEAVES - 1
-BLOCKS = 32
-PIECE = BLOCKS // 2
+PIECE = 16
 RING = N_FAR // 2
-STEPS = 7
+EVENTS = 10
+HALF_PIECE = PIECE // 2
 GROUP = 4
 GROUPS = LEAVES // GROUP
 FEATS = 16
+ROUTE = (
+    (0, 2, 1),
+    (1, 2, 1),
+    (0, 0, 2),
+    (1, 2, 2),
+    (0, 1, 2),
+    (1, 2, 3),
+    (0, 0, 3),
+    (1, 0, 4),
+    (0, 1, 3),
+    (0, 0, 4),
+)
+NEXT = {0: (2,), 1: (3, 4), 3: (5, 6), 5: (7, 8), 6: (9,)}
+AFTER_GROUP = {1: (0,), 3: (1,), 4: (2,), 7: (3,), 8: (4,), 11: (5,), 12: (6,), 15: (7,)}
 CHILD_START = (0, 64, 96, 112, 120, 124)
 ROW_START = (None, 0, 32, 48, 56, 60, 62)
 TOP_START = (0, 16, 24, 28)
@@ -84,7 +98,8 @@
     coupling,
     root_blocks,
     h0,
-    gathered,
+    level1_in,
+    upper_in,
     roots,
     tops_in,
     descent,
@@ -149,6 +164,109 @@
     load_transfer.start()
     load_coupling = pltpu.make_async_copy(coupling_hbm, coupling, load_sem.at[3])
     load_root_blocks = pltpu.make_async_copy(root_blocks_hbm, root_blocks, load_sem.at[4])
+    lax.fori_loop(0, LEAVES, wait_x, 0)
+    load_basis.wait()
+
+    def leaf_pair(q, carry):
+        parts = []
+        for t in range(2):
+            x = window[HALO + 2 * q + t, 0:RANK]
+            b = basis[:, lanes(2 * q + t)]
+            parts.append(
+                lax.dot_general(
+                    x, b, (((1,), (1,)), ((), ())), preferred_element_type=F32
+                )
+            )
+        h0[q] = jnp.concatenate(parts, axis=1).astype(BF)
+        return carry
+
+    lax.fori_loop(0, PAIRS, leaf_pair, 0, unroll=8)
+    load_transfer.wait()
+
+    def route(way, event):
+        upper, part, distance = ROUTE[event]
+        first = 0 if part == 2 else HALF_PIECE * (part ^ way)
+        count = PIECE if part == 2 else HALF_PIECE
+        return (upper_in if upper else level1_in), pl.ds(first, count), distance
+
+    def ring_copy(way, event):
+        ref, span, distance = route(way, event)
+        behind = distance - 1
+        block = ref.at[column(-behind if way == 0 else behind), span]
+        return pltpu.make_async_remote_copy(
+            src_ref=block,
+            dst_ref=block,
+            send_sem=ring_send.at[way, event],
+            recv_sem=ring_recv.at[way, event],
+            device_id=(leaf, column(1 if way == 0 else -1)),
+            device_id_type=MESH,
+        )
+
+    def sib_copy(way, event):
+        if way == 2:
+            block = (upper_in if event else level1_in).at[far]
+        else:
+            ref, span, distance = route(way, event)
+            block = ref.at[column(-distance if way == 0 else distance), span]
+        return pltpu.make_async_remote_copy(
+            src_ref=block,
+            dst_ref=block,
+            send_sem=sib_send.at[way, event],
+            recv_sem=sib_recv.at[way, event],
+            device_id=(leaf, sibling),
+            device_id_type=MESH,
+        )
+
+    def arrived(event):
+        for way in range(2):
+            ring_copy(way, event).wait_recv()
+            for later in NEXT.get(event, ()):
+                ring_copy(way, later).start()
+            sib_copy(way, event).start()
+
+    def up_level(level, sources):
+        values = []
+        for j, source in enumerate(sources):
+            first = CHILD_START[level - 1] + 2 * j
+            e = transfer[pl.ds(first, 2)].reshape(2 * RANK, RANK)
+            values.append(jnp.dot(source, e, preferred_element_type=F32) * HALF_ROOT)
+        return [
+            jnp.concatenate(values[2 * q : 2 * q + 2], axis=1).astype(BF)
+            for q in range(len(values) // 2)
+        ]
+
+    level1 = up_level(1, [h0[j] for j in range(PAIRS)])
+    for q, block in enumerate(level1):
+        level1_in[far, q] = block
+    pl.semaphore_wait(barrier, N_LEAF - 1 + N_FAR - 1)
+    ring_copy(0, 0).start()
+    ring_copy(1, 0).start()
+    sib_copy(2, 0).start()
+    blocks = level1
+    for level in range(2, 6):
+        blocks = up_level(level, blocks)
+        for q, block in enumerate(blocks):
+            upper_in[far, ROW_START[level] // 2 - PIECE + q] = block
+    e = transfer[pl.ds(CHILD_START[5], 2)].reshape(2 * RANK, RANK)
+    root = (jnp.dot(blocks[0], e, preferred_element_type=F32) * HALF_ROOT).astype(BF)
+    upper_in[far, PIECE - 1] = jnp.concatenate([root, jnp.zeros_like(root)], axis=1)
+    roots[leaf] = folded(root)
+    ring_copy(0, 1).start()
+    ring_copy(1, 1).start()
+    root_copies = []
+    for k in range(1, N_LEAF):
+        copy = pltpu.make_async_remote_copy(
+            src_ref=roots.at[leaf],
+            dst_ref=roots.at[leaf],
+            send_sem=root_send.at[k],
+            recv_sem=root_recv.at[k],
+            device_id=(leaf_peer(k), far),
+            device_id_type=MESH,
+        )
+        copy.start()
+        root_copies.append(copy)
+    sib_copy(2, 1).start()
+
     load_coupling.start()
     load_root_blocks.start()
 
@@ -171,8 +289,6 @@
         return carry
 
     lax.fori_loop(0, LEAVES * P_SIZE // chunk, make_feats, 0)
-    lax.fori_loop(0, LEAVES, wait_x, 0)
-    pl.semaphore_wait(barrier, N_LEAF - 1 + N_FAR - 1)
 
     halo = []
     for way, src in enumerate((LEAVES, HALO)):
@@ -186,98 +302,6 @@
         )
         copy.start()
         halo.append(copy)
-
-    load_basis.wait()
-
-    def leaf_pair(q, carry):
-        parts = []
-        for t in range(2):
-            x = window[HALO + 2 * q + t, 0:RANK]
-            b = basis[:, lanes(2 * q + t)]
-            parts.append(
-                lax.dot_general(
-                    x, b, (((1,), (1,)), ((), ())), preferred_element_type=F32
-                )
-            )
-        h0[q] = jnp.concatenate(parts, axis=1).astype(BF)
-        return carry
-
-    lax.fori_loop(0, PAIRS, leaf_pair, 0, unroll=8)
-    load_transfer.wait()
-
-    def piece_of(way, step):
-        return 1 - lax.rem(step, 2) if way == 1 else lax.rem(step, 2)
-
-    def ring_copy(way, step):
-        piece = piece_of(way, step)
-        behind = step // 2
-        block = gathered.at[
-            column(-behind if way == 0 else behind), pl.ds(piece * PIECE, PIECE)
-        ]
-        return pltpu.make_async_remote_copy(
-            src_ref=block,
-            dst_ref=block,
-            send_sem=ring_send.at[way, step],
-            recv_sem=ring_recv.at[way, step],
-            device_id=(leaf, column(1 if way == 0 else -1)),
-            device_id_type=MESH,
-        )
-
-    def sib_copy(way, step):
-        piece = piece_of(way, step)
-        behind = step // 2 + 1
-        part = far if way == 2 else column(-behind if way == 0 else behind)
-        block = gathered.at[part, pl.ds(piece * PIECE, PIECE)]
-        return pltpu.make_async_remote_copy(
-            src_ref=block,
-            dst_ref=block,
-            send_sem=sib_send.at[way, step],
-            recv_sem=sib_recv.at[way, step],
-            device_id=(leaf, sibling),
-            device_id_type=MESH,
-        )
-
-    def up_level(level, sources):
-        values = []
-        for j, source in enumerate(sources):
-            first = CHILD_START[level - 1] + 2 * j
-            e = transfer[pl.ds(first, 2)].reshape(2 * RANK, RANK)
-            values.append(jnp.dot(source, e, preferred_element_type=F32) * HALF_ROOT)
-        return [
-            jnp.concatenate(values[2 * q : 2 * q + 2], axis=1).astype(BF)
-            for q in range(len(values) // 2)
-        ]
-
-    level1 = up_level(1, [h0[j] for j in range(PAIRS)])
-    for q, block in enumerate(level1):
-        gathered[far, q] = block
-    ring_copy(0, 0).start()
-    ring_copy(1, 1).start()
-    sib_copy(2, 0).start()
-    blocks = level1
-    for level in range(2, 6):
-        blocks = up_level(level, blocks)
-        for q, block in enumerate(blocks):
-            gathered[far, ROW_START[level] // 2 + q] = block
-    e = transfer[pl.ds(CHILD_START[5], 2)].reshape(2 * RANK, RANK)
-    root = (jnp.dot(blocks[0], e, preferred_element_type=F32) * HALF_ROOT).astype(BF)
-    gathered[far, BLOCKS - 1] = jnp.concatenate([root, jnp.zeros_like(root)], axis=1)
-    roots[leaf] = folded(root)
-    ring_copy(0, 1).start()
-    ring_copy(1, 0).start()
-    root_copies = []
-    for k in range(1, N_LEAF):
-        copy = pltpu.make_async_remote_copy(
-            src_ref=roots.at[leaf],
-            dst_ref=roots.at[leaf],
-            send_sem=root_send.at[k],
-            recv_sem=root_recv.at[k],
-            device_id=(leaf_peer(k), far),
-            device_id_type=MESH,
-        )
-        copy.start()
-        root_copies.append(copy)
-    sib_copy(2, 1).start()
 
     def spread(q, carry):
         block = jnp.concatenate(
@@ -395,55 +419,51 @@
         p = lax.rem(step + HALO // GROUP, GROUPS)
         for t in range(GROUP):
             near_sum[:, lanes(GROUP * p + t)] = near_leaf(GROUP * p + t)
-        return carry
-
-    def segment(step, carry):
-        lax.fori_loop(
-            step * GROUPS // STEPS, (step + 1) * GROUPS // STEPS, near_group, 0
-        )
-        for way in range(2):
-            ring_copy(way, step).wait_recv()
-
-            @pl.when(step + 2 < STEPS)
+        for group, events in AFTER_GROUP.items():
+
+            @pl.when(step == group)
             def _():
-                ring_copy(way, step + 2).start()
-
-            sib_copy(way, step).start()
-
-        @pl.when(step == 0)
+                for event in events:
+                    arrived(event)
+
+        @pl.when(step == 2)
         def _():
             top_up()
             for k in range(1, N_FAR):
                 top_copy(k).start()
 
-        @pl.when(step == 2)
+        @pl.when(step == 6)
         def _():
             halo_arrived()
 
-        @pl.when(step == 3)
+        @pl.when(step == 9)
         def _():
             top_down()
 
         return carry
 
-    lax.fori_loop(0, STEPS, segment, 0)
-
-    for step in range(STEPS):
-        for way in range(2):
-            ring_copy(way, step).wait_send()
-            sib_copy(way, step).wait()
-    for piece in range(2):
-        sib_copy(2, piece).wait()
+    lax.fori_loop(0, GROUPS, near_group, 0)
     load_coupling.wait()
 
-    def gain(row):
-        half = slice((row % 2) * RANK, (row % 2 + 1) * RANK)
-        parts = [gathered[pattern[k, row], row // 2][:, half] for k in range(KC)]
+    def gain(row, parity, upper):
+        half = slice(parity * RANK, (parity + 1) * RANK)
+        ref, block = (upper_in, row // 2 - PIECE) if upper else (level1_in, row // 2)
+        parts = [ref[pattern[k, row], block][:, half] for k in range(KC)]
         return jnp.dot(
             jnp.concatenate(parts, axis=1),
             coupling[row].reshape(KC * RANK, RANK),
             preferred_element_type=F32,
         )
+
+    def others(upper):
+        events = [(2, upper)]
+        for event in range(EVENTS):
+            if ROUTE[event][0] == upper:
+                events += [(0, event), (1, event)]
+        return events
+
+    for way, event in others(1):
+        sib_copy(way, event).wait_recv()
 
     def down(level, j, value):
         start = CHILD_START[level - 1]
@@ -453,33 +473,48 @@
         )
         return both[:, :RANK], both[:, RANK:]
 
-    values = [(descent[...] + gain(NODES - 1)).astype(BF)]
+    values = [(descent[...] + gain(NODES - 1, 0, True)).astype(BF)]
     for level in range(6, 1, -1):
         children = []
         for j, value in enumerate(values):
             children += down(level, j, value)
-        values = [
-            (child + gain(ROW_START[level - 1] + j)).astype(BF)
-            for j, child in enumerate(children)
-        ]
-    for j, value in enumerate(values):
-        expansion[j] = value
+        if level > 2:
+            start = ROW_START[level - 1]
+            values = [
+                (child + gain(start + j, j % 2, True)).astype(BF)
+                for j, child in enumerate(children)
+            ]
+    for j, child in enumerate(children):
+        expansion[j] = child
+
+    for event in (8, 9):
+        arrived(event)
+    for way, event in others(0):
+        sib_copy(way, event).wait_recv()
 
     factor = 1.0 / math.sqrt(NEAR * P_SIZE)
 
-    def finish(j, carry):
-        both = down(1, j, expansion[j])
-        for t in range(2):
-            at = lanes(2 * j + t)
-            far_sum = jnp.dot(
-                both[t].astype(BF), basis[:, at], preferred_element_type=F32
-            )
-            out_vmem[:, at] = (near_sum[:, at] * factor + far_sum).astype(BF)
+    def finish(q, carry):
+        for parity in range(2):
+            j = 2 * q + parity
+            value = (expansion[j] + gain(j, parity, False)).astype(BF)
+            both = down(1, j, value)
+            for t in range(2):
+                at = lanes(2 * j + t)
+                far_sum = jnp.dot(
+                    both[t].astype(BF), basis[:, at], preferred_element_type=F32
+                )
+                out_vmem[:, at] = (near_sum[:, at] * factor + far_sum).astype(BF)
         return carry
 
-    lax.fori_loop(0, PAIRS, finish, 0, unroll=8)
+    lax.fori_loop(0, PAIRS // 2, finish, 0, unroll=8)
     store = pltpu.make_async_copy(out_vmem, out_hbm, load_sem.at[0])
     store.start()
+    for event in range(EVENTS):
+        for way in range(2):
+            ring_copy(way, event).wait_send()
+    for way, event in others(0) + others(1):
+        sib_copy(way, event).wait_send()
     store.wait()
 
 
@@ -516,21 +551,22 @@
             pltpu.VMEM((NODES, KC, RANK, RANK), BF),
             pltpu.VMEM((N_FAR, RANK, RANK), BF),
             pltpu.VMEM((PAIRS, RANK, 2 * RANK), BF),
-            pltpu.VMEM((N_FAR, BLOCKS, RANK, 2 * RANK), BF),
+            pltpu.VMEM((N_FAR, PIECE, RANK, 2 * RANK), BF),
+            pltpu.VMEM((N_FAR, PIECE, RANK, 2 * RANK), BF),
             pltpu.VMEM((N_LEAF, RANK // 2, 2 * RANK), BF),
             pltpu.VMEM((N_FAR, RANK // 2, 2 * RANK), BF),
             pltpu.VMEM((RANK, RANK), F32),
-            pltpu.VMEM((PAIRS, RANK, RANK), BF),
+            pltpu.VMEM((PAIRS, RANK, RANK), F32),
             pltpu.VMEM((RANK, points), F32),
             pltpu.VMEM((RANK, points), BF),
             dma((5,)),
             dma((LEAVES,)),
             dma((2,)),
             dma((2,)),
-            dma((2, STEPS)),
-            dma((2, STEPS)),
-            dma((3, STEPS)),
-            dma((3, STEPS)),
+            dma((2, EVENTS)),
+            dma((2, EVENTS)),
+            dma((3, EVENTS)),
+            dma((3, EVENTS)),
             dma((N_LEAF,)),
             dma((N_LEAF,)),
             dma((N_FAR,)),

time: 80.5 us -> 76.5 us (0.950)
  Pallas kernels: 73.2 us -> 69.1 us
    pallas_call x1, Pallas kernels: 73.2 us -> 69.1 us  [local(): pl.pallas_call(kernel, name='h2_product', out_shape=jax.ShapeDtypeStruct(...]
where the time goes in v3:
time: 76.5 us; the launch traced here: 76.3 us
  Pallas kernels  69.1 us (90%)
  local copies, waits for them, and re-layouts  7.18 us (9%)
    pallas_call x1, Pallas kernels, local(): pl.pallas_call(kernel, name='h2_product', out_shape=jax.ShapeDtypeStruct(...  69.1 us
    unnamed x2, local copies, waits for them, and re-layouts  7.18 us

profile of v3, /device:TPU:1, one launch (start us, length us, event | category | flops | bytes accessed | tf_op | source)
XLA Modules:
  0.0 76.3 jit_solution(12836228814271503256)
XLA Ops:
  0.0 4.9 %copy.11 = bf16[1,126,64,64]{3,2,1,0:T(8,128)(2,1)} copy(bf16[1,126,64,64]{1,3,2,0:T(8,128)(2,1)} %param.14) | data formatting | bytes 2064384 | tf_op args[4]
  4.9 69.1 %h2_product.1 = bf16[64,8192]{1,0:T(8,128)(2,1)} custom-call(s32[24,64]{1,0:T(8,128)} %bitcast.22, s32[4,63]{1,0:T(4,128)} %bitcast.23, s32[1,16]{1,0:T(1,128)} %root_pattern.1, bf16[3,8192]{1,0:T(4,128)(2,1)} %bitcast.21, bf16[30,64,64]{2,1,0:T(8,128)(2,1)} %bitcast.19, bf16[64,8192]{1,0:T(8,128)(2,1)} %bitcast.17, bf16[64,8192]{1,0:T(8,128)(2,1)} %bitcast.18, ...), custom_call_target="tpu_custom_call" | custom-call | flops 4294967296 | bytes 16777216 | tf_op jit(solution)/shard_map/h2_product/pallas_call | solution.py:538
  74.0 2.3 %copy.13 = bf16[1,64,8192]{2,1,0:T(8,128)(2,1)} copy(bf16[1,64,8192]{2,1,0:T(8,128)(2,1)} %bitcast.15) | data formatting | bytes 2097152

commit v4 on v3

--- a/solution.py
+++ b/solution.py
@@ -134,6 +134,13 @@
     def far_peer(k):
         return lax.rem(far + k + N_FAR, N_FAR)
 
+    load_rows = pltpu.make_async_copy(x_hbm, out_vmem, load_sem.at[0])
+    load_rows.start()
+    load_basis = pltpu.make_async_copy(basis_hbm, basis, load_sem.at[1])
+    load_basis.start()
+    load_transfer = pltpu.make_async_copy(transfer_hbm, transfer, load_sem.at[2])
+    load_transfer.start()
+
     barrier = pltpu.get_barrier_semaphore()
     for k in range(1, N_LEAF):
         pl.semaphore_signal(
@@ -157,20 +164,15 @@
         load_x(i).wait()
         return carry
 
-    lax.fori_loop(0, LEAVES, start_x, 0)
-    load_basis = pltpu.make_async_copy(basis_hbm, basis, load_sem.at[1])
-    load_basis.start()
-    load_transfer = pltpu.make_async_copy(transfer_hbm, transfer, load_sem.at[2])
-    load_transfer.start()
     load_coupling = pltpu.make_async_copy(coupling_hbm, coupling, load_sem.at[3])
     load_root_blocks = pltpu.make_async_copy(root_blocks_hbm, root_blocks, load_sem.at[4])
-    lax.fori_loop(0, LEAVES, wait_x, 0)
+    load_rows.wait()
     load_basis.wait()
 
     def leaf_pair(q, carry):
         parts = []
         for t in range(2):
-            x = window[HALO + 2 * q + t, 0:RANK]
+            x = out_vmem[:, lanes(2 * q + t)]
             b = basis[:, lanes(2 * q + t)]
             parts.append(
                 lax.dot_general(
@@ -242,6 +244,7 @@
     ring_copy(0, 0).start()
     ring_copy(1, 0).start()
     sib_copy(2, 0).start()
+    lax.fori_loop(0, LEAVES, start_x, 0)
     blocks = level1
     for level in range(2, 6):
         blocks = up_level(level, blocks)
@@ -290,6 +293,7 @@
 
     lax.fori_loop(0, LEAVES * P_SIZE // chunk, make_feats, 0)
 
+    lax.fori_loop(0, LEAVES, wait_x, 0)
     halo = []
     for way, src in enumerate((LEAVES, HALO)):
         copy = pltpu.make_async_remote_copy(

time: 76.5 us -> 76.4 us (level)
  no operation moved by 1% of the time
where the time goes in v4:
time: 76.4 us; the launch traced here: 76.3 us
  Pallas kernels  69.1 us (90%)
  local copies, waits for them, and re-layouts  7.18 us (9%)
    pallas_call x1, Pallas kernels, local(): pl.pallas_call(kernel, name='h2_product', out_shape=jax.ShapeDtypeStruct(...  69.1 us
    unnamed x2, local copies, waits for them, and re-layouts  7.18 us

profile of v4, /device:TPU:1, one launch (start us, length us, event | category | flops | bytes accessed | tf_op | source)
XLA Modules:
  0.0 76.3 jit_solution(3782434440120904713)
XLA Ops:
  0.0 4.9 %copy.11 = bf16[1,126,64,64]{3,2,1,0:T(8,128)(2,1)} copy(bf16[1,126,64,64]{1,3,2,0:T(8,128)(2,1)} %param.14) | data formatting | bytes 2064384 | tf_op args[4]
  4.9 69.1 %h2_product.1 = bf16[64,8192]{1,0:T(8,128)(2,1)} custom-call(s32[24,64]{1,0:T(8,128)} %bitcast.22, s32[4,63]{1,0:T(4,128)} %bitcast.23, s32[1,16]{1,0:T(1,128)} %root_pattern.1, bf16[3,8192]{1,0:T(4,128)(2,1)} %bitcast.21, bf16[30,64,64]{2,1,0:T(8,128)(2,1)} %bitcast.19, bf16[64,8192]{1,0:T(8,128)(2,1)} %bitcast.17, bf16[64,8192]{1,0:T(8,128)(2,1)} %bitcast.18, ...), custom_call_target="tpu_custom_call" | custom-call | flops 4294967296 | bytes 16777216 | tf_op jit(solution)/shard_map/h2_product/pallas_call | solution.py:542
  74.0 2.3 %copy.13 = bf16[1,64,8192]{2,1,0:T(8,128)(2,1)} copy(bf16[1,64,8192]{2,1,0:T(8,128)(2,1)} %bitcast.15) | data formatting | bytes 2097152
